TPU v7x, 512 devices: a whole 4x4x16 slice. The times are simulated.
512 devices in a mesh: dp: 128 (over x, z, core), narrow: 4 (over y).
Axes of the slice: x: 4, y: 4, z: 16, core: 2. Of those that a mesh axis runs over, the one named last changes fastest.
Arguments:
- grad_parts: bfloat16 [4, 192, 512, 512], P('narrow', None, 'dp')
- first_moment: float32 [192, 512, 512], P(None, 'dp', 'narrow'), may hold values from -320 to 320
- second_moment: float32 [192, 512, 512], P(None, 'dp', 'narrow'), may hold values from 0.25 to 4
- factors: float32 [128, 4, 512, 512], P('dp', 'narrow'), as said below
- block_order: int32 [192], replicated, may hold values from 0 to 191, each once
- owner_counts: int32 [128], replicated, may hold values from 0 to 2, as said below
Outputs:
- update: bfloat16 [192, 512, 512], P(None, 'dp', 'narrow')
- new_first: float32 [192, 512, 512], P(None, 'dp', 'narrow')
- new_second: float32 [192, 512, 512], P(None, 'dp', 'narrow')
- new_factors: float32 [128, 4, 512, 512], P('dp', 'narrow')
Inputs may be any that keep to these rules, and one draw needn't show every extreme that they name: owner_counts sum to 192; owner o's blocks are block_order[start[o]] to block_order[start[o] + owner_counts[o] - 1], with start[o] the sum of the counts of lower owners; some owner holds none and some holds 2. `factors`: every block of a statistic is symmetric, with a positive diagonal larger than the sum of magnitudes of the rest of its row.
All inputs are finite; a program needn't handle non-finite values.
Results may differ from a plain program's by a relative error of at most 0.0023.
The roundings to bfloat16 on the way count: a program that leaves them out, or rounds other values in their place, can miss the bound.
Values may be sent and summed in bfloat16 or wider, within the bound.
No kernel may reach another device: no remote copies, remote signals or barrier semaphores. Data moves between devices by JAX's collectives and lax.ppermute only.
A program may use at most 128 MiB of HBM per device.

v0:
```python
import jax
import jax.numpy as jnp
from jax import lax
from jax.sharding import PartitionSpec as P

ITERS = 2


def inverse_root(statistic):
    frob_norm = jnp.sqrt(jnp.sum(statistic * statistic))
    identity = jnp.eye(statistic.shape[0], dtype=statistic.dtype)
    current = statistic / frob_norm
    root_iter = identity
    for sweep in range(ITERS):
        step_term = (5.0 * identity - current) * 0.25
        root_iter = jnp.dot(
            root_iter,
            step_term,
            precision=lax.Precision.HIGHEST,
            preferred_element_type=jnp.float32,
        )
        squared = jnp.dot(
            step_term,
            step_term,
            precision=lax.Precision.HIGHEST,
            preferred_element_type=jnp.float32,
        )
        fourth = jnp.dot(
            squared, squared, precision=lax.Precision.HIGHEST, preferred_element_type=jnp.float32
        )
        current = jnp.dot(
            fourth, current, precision=lax.Precision.HIGHEST, preferred_element_type=jnp.float32
        )
    return root_iter * frob_norm ** (-0.25)


def slot_tables(block_order, owner_counts, slot_total):
    block_total = block_order.shape[0]
    end_points = jnp.cumsum(owner_counts)
    start_points = end_points - owner_counts
    slot_range = jnp.arange(slot_total, dtype=jnp.int32)
    filled = slot_range[None, :] < owner_counts[:, None]
    list_index = jnp.minimum(start_points[:, None] + slot_range[None, :], block_total - 1)
    blocks = block_order[list_index]
    position = (
        jnp.zeros((block_total,), jnp.int32)
        .at[block_order]
        .set(jnp.arange(block_total, dtype=jnp.int32))
    )
    owner_of = jnp.sum((end_points[None, :] <= position[:, None]).astype(jnp.int32), axis=1)
    slot_of = position - start_points[owner_of]
    return (blocks, filled, owner_of, slot_of)


def per_device(grad_parts, first_moment, second_moment, factors, block_order, owner_counts):
    owner_total = lax.axis_size("dp")
    member_total = lax.axis_size("narrow")
    owner_index = lax.axis_index("dp")
    member_index = lax.axis_index("narrow")
    slot_total = member_total // 2
    partial_value = grad_parts[0].astype(jnp.float32)
    row_count = partial_value.shape[1]
    block_size = partial_value.shape[2]
    column_count = block_size // member_total
    summed = lax.psum(partial_value, "narrow")
    gradient = lax.dynamic_slice_in_dim(summed, member_index * column_count, column_count, 2)
    new_first = 0.9 * first_moment + 0.1 * gradient
    new_second = 0.95 * second_moment + 0.05 * gradient * gradient
    adam_dir = new_first / (jnp.sqrt(new_second) + 1e-08)
    adam_sq = lax.psum(jnp.sum(adam_dir * adam_dir, axis=(1, 2)), ("dp", "narrow"))
    blocks, filled, owner_of, slot_of = slot_tables(block_order, owner_counts, slot_total)
    source = summed.astype(jnp.bfloat16)
    picked = jnp.where(filled.T[:, :, None, None], source[blocks.T], jnp.zeros((), jnp.bfloat16))
    arrived = lax.all_to_all(picked, "dp", split_axis=1, concat_axis=1, tiled=True).reshape(
        slot_total, block_size, block_size
    )
    job_slot = member_index // 2
    job_side = member_index % 2
    own_block = lax.dynamic_index_in_dim(arrived, job_slot, 0, keepdims=False)
    turned = jnp.where(job_side == 0, own_block, own_block.T)
    product = jnp.dot(turned, turned.T, preferred_element_type=jnp.float32)
    statistic = 0.9 * factors[0, 0] + 0.1 * product
    own_root = inverse_root(statistic).astype(jnp.bfloat16)
    all_roots = lax.all_gather(own_root[None], "narrow", axis=0, tiled=True)
    precond_list = []
    square_list = []
    for slot_number in range(slot_total):
        right_columns = lax.dynamic_slice_in_dim(
            all_roots[2 * slot_number + 1], member_index * column_count, column_count, 1
        )
        inner_term = jnp.dot(
            arrived[slot_number], right_columns, preferred_element_type=jnp.float32
        ).astype(jnp.bfloat16)
        precond = jnp.dot(
            all_roots[2 * slot_number], inner_term, preferred_element_type=jnp.float32
        )
        precond_list.append(precond)
        square_list.append(jnp.sum(precond * precond))
    square_totals = lax.psum(jnp.stack(square_list), "narrow")
    held_blocks = lax.dynamic_index_in_dim(blocks, owner_index, 0, keepdims=False)
    held_filled = lax.dynamic_index_in_dim(filled, owner_index, 0, keepdims=False)
    adam_norm = jnp.sqrt(jnp.where(held_filled, adam_sq[held_blocks], 0.0))
    factor_scale = adam_norm / (jnp.sqrt(square_totals) + 1e-06)
    outgoing = (jnp.stack(precond_list) * factor_scale[:, None, None]).astype(jnp.bfloat16)
    outgoing = outgoing.reshape(slot_total, owner_total, row_count, column_count)
    came_back = lax.all_to_all(outgoing, "dp", split_axis=1, concat_axis=1, tiled=True)
    returned_rows = came_back.reshape(slot_total * owner_total, row_count, column_count)
    update = returned_rows[slot_of * owner_total + owner_of]
    return (update, new_first, new_second, statistic[None, None])


def solution(mesh):
    return jax.shard_map(
        per_device,
        mesh=mesh,
        in_specs=(
            P("narrow", None, "dp", None),
            P(None, "dp", "narrow"),
            P(None, "dp", "narrow"),
            P("dp", "narrow", None, None),
            P(),
            P(),
        ),
        out_specs=(
            P(None, "dp", "narrow"),
            P(None, "dp", "narrow"),
            P(None, "dp", "narrow"),
            P("dp", "narrow", None, None),
        ),
        check_vma=False,
    )
```

profile of v0, /device:TPU:1, one launch (start us, length us, event | category | flops | bytes accessed | tf_op | source)
XLA Modules:
  0.0 337.1 jit_solution(887955641533276106)
XLA Ops:
  7.2 2.5 bitcast_convert_fusion
  10.4 1.9 gather_fusion
  12.6 68.9 %all-reduce.2.cloned.1.call-done = f32[192,4,512]{2,1,0:T(4,128)} async-done(((f32[192,4,512]{2,1,0:T(4,128)}), f32[192,4,512]{2,1,0:T(4,128)}) %all-reduce.2.cloned.1.call-update) | async-done | bytes 1572880 | tf_op jit(solution)/shard_map/psum | solution.py:65
  81.5 1.7 convert_element_type.28
  83.2 1.5 gather_fusion.1
  85.1 1.8 copy.42
  86.9 16.8 %all-to-all-start = ((bf16[2,128,4,512]{3,2,0,1:T(4,128)(2,1)}), bf16[2,128,4,512]{3,2,0,1:T(4,128)(2,1)S(1)}, u32[]{:S(2)}, u32[]{:S(2)}) async-start(bf16[2,128,4,512]{3,2,0,1:T(4,128)(2,1)} %copy.42), calls=%async_computation | async-start | bytes 2097152 | tf_op jit(solution)/shard_map/all_to_all | solution.py:74
  103.9 54.1 %all-to-all-done = bf16[2,128,4,512]{3,2,0,1:T(4,128)(2,1)S(1)} async-done(((bf16[2,128,4,512]{3,2,0,1:T(4,128)(2,1)}), bf16[2,128,4,512]{3,2,0,1:T(4,128)(2,1)S(1)}, u32[]{:S(2)}, u32[]{:S(2)}) %all-to-all-start) | async-done | bytes 1048608 | tf_op jit(solution)/shard_map/all_to_all | solution.py:74
  158.0 0.4 copy.43
  158.9 2.5 multiply_reduce_fusion
  162.1 2.0 fusion.7
  164.1 2.2 fusion.6
  166.3 1.8 fusion.48
  168.2 1.9 fusion.1
  170.1 2.7 fusion.2
  172.8 0.6 dynamic-slice.4
  173.4 2.8 multiply_reduce_fusion.1
  176.3 101.2 %psum.22 = f32[192]{0:T(256)S(1)} all-reduce(f32[192]{0:T(256)S(1)} %get-tuple-element.4), channel_id=1, replica_groups=mesh['dp'=128,'narrow'=4] {'dp','narrow'}, use_global_device_ids=true, to_apply=%region_4.5 | all-reduce | flops 192 | bytes 1536 | tf_op jit(solution)/shard_map/psum | solution.py:70
  277.5 0.4 fusion.43
  278.1 2.4 fusion.42
  280.5 2.2 multiply_reduce_fusion.2
  282.8 2.3 multiply_reduce_fusion.3
  285.0 1.3 pad_maximum_fusion
  286.4 0.6 gather_fusion.2
  287.0 7.1 %psum.23 = f32[2]{0:T(128)S(1)} all-reduce(f32[2]{0:T(128)S(1)} %pad_maximum_fusion), channel_id=1, replica_groups=mesh['dp'=128,'narrow'=4] {'narrow'}, use_global_device_ids=true, to_apply=%region_7.8 | all-reduce | flops 2 | bytes 16 | tf_op jit(solution)/shard_map/psum | solution.py:99
  294.1 0.6 fusion.31
  294.8 0.9 fusion.12
  295.6 10.5 %all-to-all-start.1 = ((bf16[2,128,4,128]{3,2,0,1:T(4,128)(2,1)}), bf16[2,128,4,128]{3,2,0,1:T(4,128)(2,1)S(1)}, u32[]{:S(2)}, u32[]{:S(2)}) async-start(bf16[2,128,4,128]{3,2,0,1:T(4,128)(2,1)} %fusion.12), calls=%async_computation.1 | async-start | bytes 524288 | tf_op jit(solution)/shard_map/all_to_all | solution.py:106
  306.2 1.2 scatter_custom_fusion
  307.6 1.6 gather_fusion.3
  309.2 19.5 %all-to-all-done.1 = bf16[2,128,4,128]{3,2,0,1:T(4,128)(2,1)S(1)} async-done(((bf16[2,128,4,128]{3,2,0,1:T(4,128)(2,1)}), bf16[2,128,4,128]{3,2,0,1:T(4,128)(2,1)S(1)}, u32[]{:S(2)}, u32[]{:S(2)}) %all-to-all-start.1) | async-done | bytes 262176 | tf_op jit(solution)/shard_map/all_to_all | solution.py:106
  328.7 1.6 gather_fusion.4
  (48 shorter events, 2.7 us)
Async XLA Ops:
  7.2 2.6 copy-start.6
  7.2 3.3 copy-start
  7.2 74.3 %all-reduce.2.cloned.1.call-start = ((), (), s32[]{:S(2)}) async-start(), calls=%async_computation.2 | async-start | bytes 3145728 | tf_op jit(solution)/shard_map/psum | solution.py:65
  86.9 71.1 %all-to-all-start = ((bf16[2,128,4,512]{3,2,0,1:T(4,128)(2,1)}), bf16[2,128,4,512]{3,2,0,1:T(4,128)(2,1)S(1)}, u32[]{:S(2)}, u32[]{:S(2)}) async-start(bf16[2,128,4,512]{3,2,0,1:T(4,128)(2,1)} %copy.42), calls=%async_computation | async-start | bytes 2097152 | tf_op jit(solution)/shard_map/all_to_all | solution.py:74
  103.6 174.5 %all-gather.3.cloned.1.call-start = ((), (), s32[]{:S(2)}) async-start(), calls=%async_computation.3 | async-start | bytes 2621440 | tf_op jit(solution)/shard_map/all_gather | solution.py:84
  161.4 6.8 %copy-start.1 = (f32[512,512]{1,0:T(8,128)}, f32[512,512]{1,0:T(8,128)S(1)}, u32[]{:S(2)}) copy-start(f32[512,512]{1,0:T(8,128)S(1)} %get-tuple-element.12) | copy-start | bytes 3145732
  168.2 1.9 copy-start.2
  170.1 3.3 copy-start.4
  170.1 3.3 copy-start.5
  278.1 2.4 copy-start.3
  295.6 33.0 %all-to-all-start.1 = ((bf16[2,128,4,128]{3,2,0,1:T(4,128)(2,1)}), bf16[2,128,4,128]{3,2,0,1:T(4,128)(2,1)S(1)}, u32[]{:S(2)}, u32[]{:S(2)}) async-start(bf16[2,128,4,128]{3,2,0,1:T(4,128)(2,1)} %fusion.12), calls=%async_computation.1 | async-start | bytes 524288 | tf_op jit(solution)/shard_map/all_to_all | solution.py:106
Sparse Core Ops, SparseCore 0:
  10.4 71.0 all-reduce.1
  172.9 31.2 all-gather.2
where the time goes:
time: 338 us; the launch traced here: 337 us
  waiting for transfers between devices  142 us (42%)
  blocking collectives  108 us (32%)
  starting transfers between devices  27.6 us (8%)
  matrix products  17.5 us (5%)
  local copies, waits for them, and re-layouts  15.5 us (5%)
  between operations  15.2 us (4%)
  other arithmetic  10.6 us (3%)
    psum x1, blocking collectives, per_device(): lax.psum(jnp.sum(adam_dir * adam_dir, axis=(1, 2)), ('dp', 'narrow'))  101 us
    psum x1, waiting for transfers between devices, per_device(): summed = lax.psum(partial_value, 'narrow')  68.9 us
    all_to_all x1, waiting for transfers between devices, per_device(): lax.all_to_all(picked, 'dp', split_axis=1, concat_axis=1, tiled=True)  54.1 us
    all_to_all x1, waiting for transfers between devices, per_device(): lax.all_to_all(outgoing, 'dp', split_axis=1, concat_axis=1, tiled=True)  19.5 us
    all_to_all x1, starting transfers between devices, per_device(): lax.all_to_all(picked, 'dp', split_axis=1, concat_axis=1, tiled=True)  16.8 us
    all_to_all x1, starting transfers between devices, per_device(): lax.all_to_all(outgoing, 'dp', split_axis=1, concat_axis=1, tiled=True)  10.5 us
    psum x1, blocking collectives, per_device(): square_totals = lax.psum(jnp.stack(square_list), 'narrow')  7.11 us
  transfers between devices with their start and end apart: 4, of which 3 were waited for; matrix products, arithmetic and copies ran while one was open for 3% of the time, Pallas kernels for 0%

commit v1 on v0

v1 whole, which is shorter than its diff:
```python
import jax
import jax.numpy as jnp
from jax import lax
from jax.experimental import pallas as pl
from jax.experimental.pallas import tpu as pltpu
from jax.sharding import PartitionSpec as P

BLOCKS = 192
OWNERS = 128
NARROW = 4
ROWS = 4
COLS = 128
ORDER = 512
GROUP = 10
BF16 = jnp.bfloat16
F32 = jnp.float32
VMEM = pl.BlockSpec(memory_space=pltpu.VMEM)
SMEM = pl.BlockSpec(memory_space=pltpu.SMEM)
POLY = (1.5625, -1101.25 / 1024.0, 781.25 / 1024.0, -312.5 / 1024.0, 62.5 / 1024.0, -6.25 / 1024.0, 0.25 / 1024.0)


def three_terms(value):
    high = value.astype(BF16).astype(F32)
    rest = value - high
    middle = rest.astype(BF16).astype(F32)
    return high, middle, (rest - middle).astype(BF16).astype(F32)


def moments_kernel(order, counts, parts, first, second, new_first, new_second, out, grads, sums, slots):
    gradient = jnp.sum(parts[...].astype(F32), axis=0)
    moment = 0.9 * first[...] + 0.1 * gradient
    new_first[...] = moment
    variance = 0.95 * second[...] + 0.05 * gradient * gradient
    new_second[...] = variance
    adam = moment / (jnp.sqrt(variance) + 1e-08)
    pairs = BLOCKS // 2
    gradient = gradient.reshape(pairs, 8, COLS)
    grads[:pairs] = gradient
    grads[pairs:, 0:4] = gradient[:, 4:8]
    grads[pairs:, 4:8] = gradient[:, 0:4]
    squares = (adam * adam).reshape(pairs, 8, COLS)
    lane = lax.broadcasted_iota(jnp.int32, (pairs, 1, COLS), 2)
    for half in range(2):
        total = jnp.sum(squares[:, 4 * half : 4 * half + 4], axis=1, keepdims=True)
        total = jnp.sum(total, axis=2, keepdims=True)
        high, middle, low = three_terms(jnp.broadcast_to(total, (pairs, 1, COLS)))
        third = jnp.where(lane >= 3, lane - 3, lane)
        sums[half] = jnp.where(third == 0, high, jnp.where(third == 1, middle, low))

    row = lax.broadcasted_iota(jnp.int32, (8, COLS), 0)
    across = lax.broadcasted_iota(jnp.int32, (1, COLS), 1)

    def four_owners(step, start):
        base = pl.multiple_of(step * (4 * GROUP), 8)
        for k in range(4):
            count = counts[step * 4 + k]
            block0 = order[jnp.minimum(start, BLOCKS - 1)]
            block1 = order[jnp.minimum(start + 1, BLOCKS - 1)]
            half0, half1 = block0 & 1, block1 & 1
            rows0 = grads[(block0 >> 1) + pairs * half0]
            rows1 = grads[(block1 >> 1) + pairs * (1 - half1)]
            both = jnp.where(row < ROWS, rows0, rows1)
            slots[pl.ds(base + GROUP * k, 8)] = jnp.where(row < ROWS * count, both, 0.0)
            totals = jnp.where(across < 3, sums[half0, block0 >> 1], sums[half1, block1 >> 1])
            totals = jnp.where(across < 3 * count, totals, 0.0)
            slots[pl.ds(base + GROUP * k + 8, 2)] = jnp.broadcast_to(totals, (2, COLS))
            start = start + count
        return start

    lax.fori_loop(0, OWNERS // 4, four_owners, jnp.int32(0))
    out[...] = slots[...].astype(BF16)


def spread_kernel(arrived, out, wide, halves):
    wide[...] = arrived[...].astype(F32)

    def four_sources(step, total):
        base = pl.multiple_of(step * (4 * GROUP), 8)
        for k in range(4):
            at = base + GROUP * k
            halves[0, pl.ds(step * 16 + ROWS * k, ROWS)] = wide[pl.ds(at, ROWS)]
            halves[1, pl.ds(step * 16 + ROWS * k, ROWS)] = wide[pl.ds(at + ROWS, ROWS)]
            total = total + wide[pl.ds(at + 8, 1)]
        return total

    total = lax.fori_loop(0, OWNERS // 4, four_sources, jnp.zeros((1, COLS), F32))
    across = lax.broadcasted_iota(jnp.int32, (1, COLS), 1)
    for slot in range(2):
        block = halves[slot].astype(BF16)
        mine = (across >= 3 * slot) & (across < 3 * slot + 3)
        sum_sq = jnp.sum(jnp.where(mine, total, 0.0), axis=1, keepdims=True)
        high, middle, low = three_terms(jnp.broadcast_to(sum_sq, (1, COLS)))
        pieces = jnp.where(across == 0, high, jnp.where(across == 1, middle, jnp.where(across == 2, low, 0.0)))
        pieces = jnp.broadcast_to(pieces, (16, COLS)).astype(BF16)
        for member in (2 * slot, 2 * slot + 1):
            out[member, 0:ORDER] = block
            out[member, ORDER : ORDER + 16] = pieces


def product(left, right, contract):
    return lax.dot_general(left, right, (contract, ((), ())), preferred_element_type=F32)


def two_terms(value):
    high = value.astype(BF16)
    return high, (value - high.astype(F32)).astype(BF16)


def float_product(left, right):
    high0, low0 = left
    high1, low1 = right
    plain = ((1,), (0,))
    return product(high0, high1, plain) + (product(high0, low1, plain) + product(low0, high1, plain))


def root_of(statistic):
    norm = jnp.sqrt(jnp.sum(jnp.sum(statistic * statistic, axis=0, keepdims=True), axis=1, keepdims=True))
    matrix = statistic / norm
    matrix_terms = two_terms(matrix)
    square = float_product(matrix_terms, matrix_terms)
    cube = float_product(matrix_terms, two_terms(square))
    above = POLY[4] * matrix + POLY[5] * square + POLY[6] * cube
    top = float_product(two_terms(cube), two_terms(above))
    row = lax.broadcasted_iota(jnp.int32, (ORDER, ORDER), 0)
    col = lax.broadcasted_iota(jnp.int32, (ORDER, ORDER), 1)
    value = POLY[1] * matrix + POLY[2] * square + (POLY[3] * cube + top)
    value = value + jnp.where(row == col, POLY[0], 0.0)
    return (value * lax.rsqrt(jnp.sqrt(norm))).astype(BF16)


def owner_kernel(member_ref, chunks, mine, other, new_mine, kept, passed, grad, turned, left, right, result):
    member = member_ref[0]
    is_right = (member & 1) == 1
    for n in range(NARROW):
        grad[:, COLS * n : COLS * (n + 1)] = chunks[n, 0:ORDER]
    adam_sq = jnp.zeros((1, COLS), F32)
    for n in range(NARROW):
        adam_sq = adam_sq + chunks[n, ORDER : ORDER + 16].astype(F32)[0:1]
    adam_sq = jnp.sum(adam_sq, axis=1, keepdims=True)

    def sides(left_factor, right_factor):
        block = grad[...]
        left_stat = 0.9 * left_factor[...] + 0.1 * product(block, block, ((1,), (1,)))
        left[...] = root_of(left_stat)
        right_stat = 0.9 * right_factor[...] + 0.1 * product(block, block, ((0,), (0,)))
        right[...] = root_of(right_stat)
        return left_stat, right_stat

    @pl.when(jnp.logical_not(is_right))
    def _():
        new_mine[...] = sides(mine, other)[0]

    @pl.when(is_right)
    def _():
        new_mine[...] = sides(other, mine)[1]

    inner = product(grad[...], right[...], ((1,), (0,))).astype(BF16)
    precond = product(left[...], inner, ((1,), (0,)))
    square = jnp.sum(jnp.sum(precond * precond, axis=0, keepdims=True), axis=1, keepdims=True)
    scale = jnp.sqrt(adam_sq) / (jnp.sqrt(square) + 1e-06)
    result[...] = precond * scale
    kept[...] = result[:, pl.ds(pl.multiple_of(member * COLS, COLS), COLS)].astype(BF16)
    passed[...] = result[:, pl.ds(pl.multiple_of((NARROW - 1 - member) * COLS, COLS), COLS)].astype(BF16)


def place_kernel(order, counts, member_ref, arrived, update, wide, blocks):
    wide[...] = arrived[...].astype(F32).reshape(2, OWNERS // 2, 8, COLS)
    flip = member_ref[0] >> 1

    def two_owners(step, start):
        for k in range(2):
            count = counts[step * 2 + k]
            for slot in range(2):
                rows = wide[slot ^ flip, step, ROWS * k : ROWS * (k + 1)]
                filled = count > slot
                block = order[jnp.minimum(start + slot, BLOCKS - 1)]
                blocks[jnp.where(filled, block, BLOCKS), 0:ROWS] = rows
            start = start + count
        return start

    lax.fori_loop(0, OWNERS // 2, two_owners, jnp.int32(0))
    packed = blocks[0:BLOCKS].reshape(BLOCKS // 2, 2, 8, COLS)
    joined = jnp.concatenate([packed[:, 0, 0:ROWS], packed[:, 1, 0:ROWS]], axis=1)
    update[...] = joined.reshape(BLOCKS * ROWS, COLS).astype(BF16)


def call(kernel, in_specs, out_shapes, scratch, vmem_mib, flops, moved):
    return pl.pallas_call(
        kernel,
        in_specs=in_specs,
        out_specs=[VMEM] * len(out_shapes),
        out_shape=out_shapes,
        scratch_shapes=scratch,
        compiler_params=pltpu.CompilerParams(vmem_limit_bytes=vmem_mib * 1024 * 1024),
        cost_estimate=pl.CostEstimate(flops=flops, bytes_accessed=moved, transcendentals=0),
    )


def per_device(grad_parts, first_moment, second_moment, factors, block_order, owner_counts):
    member = lax.axis_index("narrow").astype(jnp.int32).reshape(1)
    shape = jax.ShapeDtypeStruct
    flat = BLOCKS * ROWS

    partial_cols = grad_parts[0].reshape(BLOCKS, ROWS, NARROW, COLS).transpose(2, 0, 1, 3)
    partial_cols = lax.all_to_all(partial_cols, "narrow", 0, 0, tiled=True)

    factor, partial_cols = lax.optimization_barrier((factors[0, 0], partial_cols))
    other_factor = lax.ppermute(factor, "narrow", [(0, 1), (1, 0), (2, 3), (3, 2)])

    new_first, new_second, outgoing = call(
        moments_kernel,
        [SMEM, SMEM, VMEM, VMEM, VMEM],
        [shape((flat, COLS), F32), shape((flat, COLS), F32), shape((OWNERS * GROUP, COLS), BF16)],
        [
            pltpu.VMEM((BLOCKS, 8, COLS), F32),
            pltpu.VMEM((2, BLOCKS // 2, 1, COLS), F32),
            pltpu.VMEM((OWNERS * GROUP, COLS), F32),
        ],
        16,
        4_000_000,
        2_800_000,
    )(
        block_order,
        owner_counts,
        partial_cols.reshape(NARROW, flat, COLS),
        first_moment.reshape(flat, COLS),
        second_moment.reshape(flat, COLS),
    )

    arrived = lax.all_to_all(outgoing.reshape(OWNERS, GROUP // 2, 2, COLS), "dp", 0, 0, tiled=True)
    (spread,) = call(
        spread_kernel,
        [VMEM],
        [shape((NARROW, ORDER + 16, COLS), BF16)],
        [pltpu.VMEM((OWNERS * GROUP, COLS), F32), pltpu.VMEM((2, ORDER, COLS), F32)],
        16,
        1_000_000,
        900_000,
    )(arrived.reshape(OWNERS * GROUP, COLS))
    chunks = lax.all_to_all(spread, "narrow", 0, 0, tiled=True)

    new_factor, kept, passed = call(
        owner_kernel,
        [SMEM, VMEM, VMEM, VMEM],
        [shape((ORDER, ORDER), F32), shape((ORDER, COLS), BF16), shape((ORDER, COLS), BF16)],
        [pltpu.VMEM((ORDER, ORDER), BF16)] * 4 + [pltpu.VMEM((ORDER, ORDER), F32)],
        40,
        6_000_000_000,
        4_000_000,
    )(member, chunks, factor, other_factor)

    received = lax.ppermute(passed, "narrow", [(0, 3), (3, 0), (1, 2), (2, 1)])
    outgoing = jnp.stack([kept, received]).reshape(2, OWNERS, ROWS, COLS)
    came_back = lax.all_to_all(outgoing, "dp", 1, 1, tiled=True)
    (update,) = call(
        place_kernel,
        [SMEM, SMEM, SMEM, VMEM],
        [shape((flat, COLS), BF16)],
        [pltpu.VMEM((2, OWNERS // 2, 8, COLS), F32), pltpu.VMEM((BLOCKS + 8, 8, COLS), F32)],
        16,
        1_000_000,
        500_000,
    )(block_order, owner_counts, member, came_back.reshape(2, ORDER, COLS))
    local = (BLOCKS, ROWS, COLS)
    return update.reshape(local), new_first.reshape(local), new_second.reshape(local), new_factor[None, None]


def solution(mesh):
    return jax.shard_map(
        per_device,
        mesh=mesh,
        in_specs=(
            P("narrow", None, "dp", None),
            P(None, "dp", "narrow"),
            P(None, "dp", "narrow"),
            P("dp", "narrow", None, None),
            P(),
            P(),
        ),
        out_specs=(
            P(None, "dp", "narrow"),
            P(None, "dp", "narrow"),
            P(None, "dp", "narrow"),
            P("dp", "narrow", None, None),
        ),
        check_vma=False,
    )
```

time: 338 us -> 136 us (0.40)
  waiting for transfers between devices: 142 us -> 34.9 us
  blocking collectives: 108 us -> 48.7 us
  matrix products: 17.5 us -> 0 us
  Pallas kernels: 0 us -> 15.6 us
  between operations: 15.2 us -> 0.74 us
  local copies, waits for them, and re-layouts: 15.5 us -> 2.93 us
  other arithmetic: 10.6 us -> 0.19 us
  starting transfers between devices: 27.6 us -> 32.2 us
    psum x2 -> x0, blocking collectives: 108 us -> none  [the longest x1 101 us: per_device(): lax.psum(jnp.sum(adam_dir * adam_dir, axis=(1, 2)), ('dp', 'narrow'))]
    psum x1 -> x0, waiting for transfers between devices: 68.9 us -> none  [per_device(): summed = lax.psum(partial_value, 'narrow')]
    all_to_all x0 -> x2, blocking collectives: none -> 48.7 us  [the longest x1 35.5 us: per_device(): came_back = lax.all_to_all(outgoing, 'dp', 1, 1, tiled=True)]
    all_to_all x2, waiting for transfers between devices: 73.6 us -> 30.7 us  [the longest x1 23.2 us: per_device(): lax.all_to_all(outgoing.reshape(OWNERS, GROUP // 2, 2, COLS), 'dp', 0, 0,...]
    dot_general x8 -> x0, matrix products: 17.5 us -> none  [the longest x2 4.85 us: inverse_root(): jnp.dot(root_iter, step_term, precision=lax.Precision.HIGHEST, preferred_...]
    pallas_call x0 -> x4, Pallas kernels: none -> 15.6 us  [the longest x1 8.55 us: per_device(): call(owner_kernel, [SMEM, VMEM, VMEM, VMEM], [shape((ORDER, ORDER), F32),...]
    gather x7 -> x0, local copies, waits for them, and re-layouts: 7.55 us -> none  [the longest x2 2.08 us: slot_tables(): blocks = block_order[list_index]]
    convert_element_type x3 -> x0, other arithmetic: 5.05 us -> none  [the longest x1 2.51 us: per_device(): partial_value = grad_parts[0].astype(jnp.float32)]
  transfers between devices with their start and end apart: 4 -> 4, of which waited for: 3 -> 3; matrix products, arithmetic and copies ran while one was open for 3% -> 0% of each run, Pallas kernels for 0% -> 1%
where the time goes in v1:
time: 136 us; the launch traced here: 135 us
  blocking collectives  48.7 us (36%)
  waiting for transfers between devices  34.9 us (26%)
  starting transfers between devices  32.2 us (24%)
  Pallas kernels  15.6 us (11%)
  local copies, waits for them, and re-layouts  2.93 us (2%)
    all_to_all x1, blocking collectives, per_device(): came_back = lax.all_to_all(outgoing, 'dp', 1, 1, tiled=True)  35.5 us
    all_to_all x1, starting transfers between devices, per_device(): lax.all_to_all(outgoing.reshape(OWNERS, GROUP // 2, 2, COLS), 'dp', 0, 0,...  23.8 us
    all_to_all x1, waiting for transfers between devices, per_device(): lax.all_to_all(outgoing.reshape(OWNERS, GROUP // 2, 2, COLS), 'dp', 0, 0,...  23.2 us
    all_to_all x1, blocking collectives, per_device(): partial_cols = lax.all_to_all(partial_cols, 'narrow', 0, 0, tiled=True)  13.3 us
    pallas_call x1, Pallas kernels, per_device(): call(owner_kernel, [SMEM, VMEM, VMEM, VMEM], [shape((ORDER, ORDER), F32),...  8.55 us
    all_to_all x1, waiting for transfers between devices, per_device(): chunks = lax.all_to_all(spread, 'narrow', 0, 0, tiled=True)  7.53 us
    ppermute x1, waiting for transfers between devices, per_device(): received = lax.ppermute(passed, 'narrow', [(0, 3), (3, 0), (1, 2), (2, 1)])  4.21 us
    all_to_all x1, starting transfers between devices, per_device(): chunks = lax.all_to_all(spread, 'narrow', 0, 0, tiled=True)  3.47 us
  transfers between devices with their start and end apart: 4, of which 3 were waited for; matrix products, arithmetic and copies ran while one was open for 0% of the time, Pallas kernels for 1%

profile of v1, /device:TPU:1, one launch (start us, length us, event | category | flops | bytes accessed | tf_op | source)
XLA Modules:
  0.0 135.3 jit_solution(11710158350723520065)
XLA Ops:
  0.6 1.8 %reshape_squeeze.3 = bf16[192,4,4,128]{3,2,1,0:T(4,128)(2,1)S(1)} reshape(bf16[1,192,4,512]{3,2,1,0:T(4,128)(2,1)} %param.6) | data formatting | bytes 1572864 | tf_op jit(solution)/shard_map/reshape;squeeze | solution.py:204
  2.5 0.3 copy.16
  2.8 0.0 copy-start
  2.8 0.0 copy-start.1
  2.8 13.3 %all_to_all.20 = bf16[4,192,4,128]{3,2,1,0:T(4,128)(2,1)S(1)} all-to-all(bf16[4,192,4,128]{3,2,1,0:T(4,128)(2,1)S(1)} %bitcast.29), channel_id=1, replica_groups=mesh['dp'=128,'narrow'=4] {'narrow'}, dimensions={0} | all-to-all | bytes 1572864 | tf_op jit(solution)/shard_map/all_to_all | solution.py:205
  16.1 0.0 copy-start.2
  16.1 0.0 copy-start.3
  16.1 0.0 copy-done
  16.1 0.0 copy-done.1
  16.1 0.7 copy-done.2
  16.8 0.0 copy-done.3
  16.8 0.0 copy-start.4
  16.8 3.5 %shard_map.93 = (f32[768,128]{1,0:T(8,128)}, f32[768,128]{1,0:T(8,128)}, bf16[1280,128]{1,0:T(8,128)(2,1)}) custom-call(s32[192]{0:T(256)S(1)} %copy-done.2, s32[128]{0:T(128)S(1)} %copy-done.3, bf16[4,768,128]{2,1,0:T(8,128)(2,1)S(1)} %bitcast.21, f32[768,128]{1,0:T(8,128)S(1)} %bitcast.24, f32[768,128]{1,0:T(8,128)S(1)} %bitcast.25), custom_call_target="tpu_custom_call" | custom-call | flops 4000000 | bytes 2800000 | tf_op jit(solution)/shard_map/pallas_call | solution.py:210
  20.3 23.8 %all-to-all-start.1 = ((bf16[128,5,2,128]{3,2,1,0:T(2,128)(2,1)}), bf16[128,5,2,128]{3,2,1,0:T(2,128)(2,1)S(1)}, u32[]{:S(2)}, u32[]{:S(2)}) async-start(bf16[128,5,2,128]{3,2,1,0:T(2,128)(2,1)} %bitcast.6), calls=%async_computation.1 | async-start | bytes 655360 | tf_op jit(solution)/shard_map/all_to_all | solution.py:230
  44.1 0.0 copy-done.4
  44.1 2.2 %collective-permute-start = (f32[512,512]{1,0:T(8,128)S(1)}, f32[512,512]{1,0:T(8,128)S(1)}, u32[]{:S(2)}, u32[]{:S(2)}) collective-permute-start(f32[512,512]{1,0:T(8,128)S(1)} %bitcast.27), channel_id=1, source_target_pairs={{0,1},{1,0},{2,3},{3,2},{4,5},{5,4},{6,7},{7,6},{8,9},{9,8},{10,11... | collective-permute-start | bytes 3145736 | tf_op jit(solution)/shard_map/ppermute | solution.py:208
  46.3 23.2 %all-to-all-done.1 = bf16[128,5,2,128]{3,2,1,0:T(2,128)(2,1)S(1)} async-done(((bf16[128,5,2,128]{3,2,1,0:T(2,128)(2,1)}), bf16[128,5,2,128]{3,2,1,0:T(2,128)(2,1)S(1)}, u32[]{:S(2)}, u32[]{:S(2)}) %all-to-all-start.1) | async-done | bytes 327712 | tf_op jit(solution)/shard_map/all_to_all | solution.py:230
  69.5 1.3 shard_map.94
  70.7 3.5 %all-to-all-start.2 = ((bf16[4,528,128]{2,1,0:T(8,128)(2,1)}), bf16[4,528,128]{2,1,0:T(8,128)(2,1)S(1)}, u32[]{:S(2)}, u32[]{:S(2)}) async-start(bf16[4,528,128]{2,1,0:T(8,128)(2,1)} %shard_map.94), calls=%async_computation.2 | async-start | bytes 1081344 | tf_op jit(solution)/shard_map/all_to_all | solution.py:240
  74.2 0.0 collective-permute-done.other
  74.2 7.5 %all-to-all-done.2.chunks = bf16[4,528,128]{2,1,0:T(8,128)(2,1)S(1)} async-done(((bf16[4,528,128]{2,1,0:T(8,128)(2,1)}), bf16[4,528,128]{2,1,0:T(8,128)(2,1)S(1)}, u32[]{:S(2)}, u32[]{:S(2)}) %all-to-all-start.2) | async-done | bytes 540704 | tf_op jit(solution)/shard_map/all_to_all | solution.py:240
  81.7 8.6 %shard_map.95 = (f32[512,512]{1,0:T(8,128)}, bf16[512,128]{1,0:T(8,128)(2,1)S(1)}, bf16[512,128]{1,0:T(8,128)(2,1)S(1)}) custom-call(s32[1]{0:T(128)} %bitcast.member_ref, bf16[4,528,128]{2,1,0:T(8,128)(2,1)S(1)} %all-to-all-done.2.chunks, f32[512,512]{1,0:T(8,128)S(1)} %bitcast.28, f32[512,512]{1,0:T(8,128)S(1)} %collective-permute-done.other), custom_call_target="tpu_custom_call" | custom-call | flops 6000000000 | bytes 4000000 | tf_op jit(solution)/shard_map/pallas_call | solution.py:242
  90.3 2.7 %collective-permute-start.1 = (bf16[512,128]{1,0:T(8,128)(2,1)S(1)}, bf16[512,128]{1,0:T(8,128)(2,1)S(1)}, u32[]{:S(2)}, u32[]{:S(2)}) collective-permute-start(bf16[512,128]{1,0:T(8,128)(2,1)S(1)} %get-tuple-element.16), channel_id=1, source_target_pairs={{0,3},{3,0},{1,2},{2,1},{4,7},{7,4},{5,6},{6,5},{8,11},{11,8},{9,1... | collective-permute-start | bytes 393224 | tf_op jit(solution)/shard_map/ppermute | solution.py:252
  93.0 4.2 %collective-permute-done.1 = bf16[512,128]{1,0:T(8,128)(2,1)S(1)} collective-permute-done((bf16[512,128]{1,0:T(8,128)(2,1)S(1)}, bf16[512,128]{1,0:T(8,128)(2,1)S(1)}, u32[]{:S(2)}, u32[]{:S(2)}) %collective-permute-start.1) | collective-permute-done | bytes 131104 | tf_op jit(solution)/shard_map/ppermute | solution.py:252
  97.2 0.2 pad_maximum_fusion
  97.4 35.5 %all_to_all.21 = bf16[2,128,4,128]{3,2,0,1:T(4,128)(2,1)S(1)} all-to-all(bf16[2,128,4,128]{3,2,0,1:T(4,128)(2,1)S(1)} %pad_maximum_fusion), channel_id=1, replica_groups=mesh['dp'=128,'narrow'=4] {'dp'}, dimensions={1} | all-to-all | bytes 524288 | tf_op jit(solution)/shard_map/all_to_all | solution.py:254
  132.9 0.1 copy.14
  133.0 2.3 %shard_map.96 = bf16[768,128]{1,0:T(8,128)(2,1)} custom-call(s32[192]{0:T(256)S(1)} %copy-done.2, s32[128]{0:T(128)S(1)} %copy-done.3, s32[1]{0:T(128)} %bitcast.member_ref, bf16[2,512,128]{2,1,0:T(8,128)(2,1)S(1)} %bitcast.23), custom_call_target="tpu_custom_call" | custom-call | flops 1000000 | bytes 500000 | tf_op jit(solution)/shard_map/pallas_call | solution.py:255
Async XLA Ops:
  2.8 13.3 %copy-start = (f32[192,4,128]{2,1,0:T(4,128)S(1)}, f32[192,4,128]{2,1,0:T(4,128)}, u32[]{:S(2)}) copy-start(f32[192,4,128]{2,1,0:T(4,128)} %param.7) | copy-start | bytes 1179652
  2.8 13.3 %copy-start.1 = (f32[192,4,128]{2,1,0:T(4,128)S(1)}, f32[192,4,128]{2,1,0:T(4,128)}, u32[]{:S(2)}) copy-start(f32[192,4,128]{2,1,0:T(4,128)} %param.8) | copy-start | bytes 1179652
  16.1 0.7 copy-start.2
  16.1 0.7 copy-start.3
  16.8 27.3 %copy-start.4 = (f32[1,1,512,512]{3,2,1,0:T(8,128)S(1)}, f32[1,1,512,512]{3,2,1,0:T(8,128)}, u32[]{:S(2)}) copy-start(f32[1,1,512,512]{3,2,1,0:T(8,128)} %param.9) | copy-start | bytes 3145732
  20.3 49.2 %all-to-all-start.1 = ((bf16[128,5,2,128]{3,2,1,0:T(2,128)(2,1)}), bf16[128,5,2,128]{3,2,1,0:T(2,128)(2,1)S(1)}, u32[]{:S(2)}, u32[]{:S(2)}) async-start(bf16[128,5,2,128]{3,2,1,0:T(2,128)(2,1)} %bitcast.6), calls=%async_computation.1 | async-start | bytes 655360 | tf_op jit(solution)/shard_map/all_to_all | solution.py:230
  44.1 30.1 %collective-permute-start = (f32[512,512]{1,0:T(8,128)S(1)}, f32[512,512]{1,0:T(8,128)S(1)}, u32[]{:S(2)}, u32[]{:S(2)}) collective-permute-start(f32[512,512]{1,0:T(8,128)S(1)} %bitcast.27), channel_id=1, source_target_pairs={{0,1},{1,0},{2,3},{3,2},{4,5},{5,4},{6,7},{7,6},{8,9},{9,8},{10,11... | collective-permute-start | bytes 3145736 | tf_op jit(solution)/shard_map/ppermute | solution.py:208
  70.7 11.0 %all-to-all-start.2 = ((bf16[4,528,128]{2,1,0:T(8,128)(2,1)}), bf16[4,528,128]{2,1,0:T(8,128)(2,1)S(1)}, u32[]{:S(2)}, u32[]{:S(2)}) async-start(bf16[4,528,128]{2,1,0:T(8,128)(2,1)} %shard_map.94), calls=%async_computation.2 | async-start | bytes 1081344 | tf_op jit(solution)/shard_map/all_to_all | solution.py:240
  90.3 6.9 %collective-permute-start.1 = (bf16[512,128]{1,0:T(8,128)(2,1)S(1)}, bf16[512,128]{1,0:T(8,128)(2,1)S(1)}, u32[]{:S(2)}, u32[]{:S(2)}) collective-permute-start(bf16[512,128]{1,0:T(8,128)(2,1)S(1)} %get-tuple-element.16), channel_id=1, source_target_pairs={{0,3},{3,0},{1,2},{2,1},{4,7},{7,4},{5,6},{6,5},{8,11},{11,8},{9,1... | collective-permute-start | bytes 393224 | tf_op jit(solution)/shard_map/ppermute | solution.py:252

commit v2 on v1

v2 whole, which is shorter than its diff:
```python
import jax
import jax.numpy as jnp
from jax import lax
from jax.experimental import pallas as pl
from jax.experimental.pallas import tpu as pltpu
from jax.sharding import PartitionSpec as P

BLOCKS = 192
OWNERS = 128
NARROW = 4
ROWS = 4
COLS = 128
ORDER = 512
GROUP = 10
BF16 = jnp.bfloat16
F32 = jnp.float32
VMEM = pl.BlockSpec(memory_space=pltpu.VMEM)
SMEM = pl.BlockSpec(memory_space=pltpu.SMEM)
ANY = pl.BlockSpec(memory_space=pl.ANY)
PAIRS = BLOCKS // 2
EMPTY = BLOCKS
POLY = (1.5625, -1101.25 / 1024.0, 781.25 / 1024.0, -312.5 / 1024.0, 62.5 / 1024.0, -6.25 / 1024.0, 0.25 / 1024.0)


def three_terms(value):
    high = value.astype(BF16).astype(F32)
    rest = value - high
    middle = rest.astype(BF16).astype(F32)
    return high, middle, (rest - middle).astype(BF16).astype(F32)


def columns_kernel(parts, out, sem):
    copies = [
        pltpu.make_async_copy(parts.at[:, :, pl.ds(COLS * n, COLS)], out.at[n], sem.at[n]) for n in range(NARROW)
    ]
    for copy in copies:
        copy.start()
    for copy in copies:
        copy.wait()


def table_kernel(order, counts, table):
    def step(index, start):
        for k in range(8):
            owner = index * 8 + k
            count = counts[owner]
            for slot in range(2):
                block = order[jnp.minimum(start + slot, BLOCKS - 1)]
                filled = count > slot
                half = (block & 1) if slot == 0 else 1 - (block & 1)
                table[slot * OWNERS + owner] = jnp.where(filled, (block >> 1) + PAIRS * half, EMPTY)
                table[(2 + slot) * OWNERS + owner] = jnp.where(filled, block, EMPTY)
            start = start + count
        return start

    lax.fori_loop(0, OWNERS // 8, step, jnp.int32(0))


def moments_kernel(
    table, parts, first, second, new_first, new_second, out, entries, slots, moment_held, variance_held, sem
):
    gradient = jnp.sum(parts[...].astype(F32), axis=0)
    moment = 0.9 * first[...] + 0.1 * gradient
    variance = 0.95 * second[...] + 0.05 * gradient * gradient
    moment_held[...] = moment
    variance_held[...] = variance
    copies = [
        pltpu.make_async_copy(moment_held, new_first, sem.at[0]),
        pltpu.make_async_copy(variance_held, new_second, sem.at[1]),
    ]
    for copy in copies:
        copy.start()
    adam = moment / (jnp.sqrt(variance) + 1e-08)
    gradient = gradient.reshape(PAIRS, 8, COLS)
    entries[:PAIRS, 0:8] = gradient
    entries[PAIRS : 2 * PAIRS, 0:4] = gradient[:, 4:8]
    entries[PAIRS : 2 * PAIRS, 4:8] = gradient[:, 0:4]
    squares = (adam * adam).reshape(PAIRS, 8, COLS)
    upper = lax.broadcasted_iota(jnp.int32, (1, 8, COLS), 1) < ROWS
    fore = lax.broadcasted_iota(jnp.int32, (1, 8, COLS), 2) < 3
    row_sums = jnp.sum(squares, axis=2, keepdims=True)
    lane = lax.broadcasted_iota(jnp.int32, (1, 1, COLS), 2)
    term = jnp.where(lane >= 3, lane - 3, lane)
    for half in range(2):
        pick = (upper == fore) if half == 0 else (upper != fore)
        total = jnp.sum(jnp.where(pick, row_sums, 0.0), axis=1, keepdims=True)
        high, middle, low = three_terms(total)
        pieces = jnp.where(term == 0, high, jnp.where(term == 1, middle, low))
        entries[PAIRS * half : PAIRS * (half + 1), 8:9] = pieces
    entries[EMPTY] = jnp.zeros((16, COLS), F32)
    row = lax.broadcasted_iota(jnp.int32, (8, COLS), 0)
    across = lax.broadcasted_iota(jnp.int32, (1, COLS), 1)

    def four_owners(step, carry):
        base = pl.multiple_of(step * (4 * GROUP), 8)
        for k in range(4):
            entry0 = table[step * 4 + k]
            entry1 = table[OWNERS + step * 4 + k]
            slots[pl.ds(base + GROUP * k, 8)] = jnp.where(row < ROWS, entries[entry0, 0:8], entries[entry1, 0:8])
            totals = jnp.where(across < 3, entries[entry0, 8:9], entries[entry1, 8:9])
            slots[pl.ds(base + GROUP * k + 8, 2)] = jnp.broadcast_to(totals, (2, COLS))
        return carry

    lax.fori_loop(0, OWNERS // 4, four_owners, 0)
    out[...] = slots[...].astype(BF16)
    for copy in copies:
        copy.wait()


def spread_kernel(arrived, out):
    groups = arrived[...].astype(F32).reshape(OWNERS // 4, 4 * GROUP, COLS)
    starts = [GROUP * k for k in range(4)]
    total = jnp.sum(sum(groups[:, at + 8 : at + 9] for at in starts), axis=0)
    across = lax.broadcasted_iota(jnp.int32, (1, COLS), 1)
    for slot in range(2):
        rows = [groups[:, at + ROWS * slot : at + ROWS * (slot + 1)] for at in starts]
        block = jnp.concatenate(rows, axis=1).reshape(ORDER, COLS).astype(BF16)
        mine = (across >= 3 * slot) & (across < 3 * slot + 3)
        sum_sq = jnp.sum(jnp.where(mine, total, 0.0), axis=1, keepdims=True)
        high, middle, low = three_terms(jnp.broadcast_to(sum_sq, (1, COLS)))
        pieces = jnp.where(across == 0, high, jnp.where(across == 1, middle, jnp.where(across == 2, low, 0.0)))
        pieces = jnp.broadcast_to(pieces, (16, COLS)).astype(BF16)
        for member in (2 * slot, 2 * slot + 1):
            out[member, 0:ORDER] = block
            out[member, ORDER : ORDER + 16] = pieces


def product(left, right, contract=((1,), (0,))):
    return lax.dot_general(left, right, (contract, ((), ())), preferred_element_type=F32)


def two_terms(value):
    high = value.astype(BF16)
    return high, (value - high.astype(F32)).astype(BF16)


def sum_of_squares(parts):
    total = sum(jnp.sum((part * part).reshape(-1, 8, ORDER), axis=0) for part in parts)
    return jnp.sum(jnp.sum(total, axis=0, keepdims=True), axis=1, keepdims=True)


def owner_kernel(
    member_ref, chunks, mine, other, new_mine, kept, passed, grad, stats, lefts, rights, later, squares, outer, cubes, roots, inner, result
):
    member = member_ref[0]
    is_right = (member & 1) == 1
    halves = [slice(0, ORDER // 2), slice(ORDER // 2, ORDER)]
    for n in range(NARROW):
        grad[:, COLS * n : COLS * (n + 1)] = chunks[n, 0:ORDER]
    adam_sq = sum(chunks[n, ORDER : ORDER + 16].astype(F32)[0:1] for n in range(NARROW))
    adam_sq = jnp.sum(adam_sq, axis=1, keepdims=True)

    def statistics(left_factor, right_factor, side):
        for rows in halves:
            left = 0.9 * left_factor[rows].astype(F32) + 0.1 * product(grad[rows], grad[...], ((1,), (1,)))
            stats[0, rows] = left
            if side == 0:
                new_mine[rows] = left
        for rows in halves:
            right = 0.9 * right_factor[rows].astype(F32) + 0.1 * product(grad[:, rows], grad[...], ((0,), (0,)))
            stats[1, rows] = right
            if side == 1:
                new_mine[rows] = right

    @pl.when(jnp.logical_not(is_right))
    def _():
        statistics(mine, other, 0)

    @pl.when(is_right)
    def _():
        statistics(other, mine, 1)

    norms = [jnp.sqrt(sum_of_squares([stats[side, rows] for rows in halves])) for side in range(2)]
    inverses = [1.0 / norm for norm in norms]

    def put_right(target, side, rows, high, low):
        for third, term in enumerate((high, low, high)):
            target[side, third * ORDER + rows.start : third * ORDER + rows.stop] = term

    for side in range(2):
        for rows in halves:
            high, low = two_terms(stats[side, rows] * inverses[side])
            for third, term in enumerate((high, high, low)):
                lefts[side, rows, third * ORDER : (third + 1) * ORDER] = term
            put_right(rights, side, rows, high, low)
    for side in range(2):
        for rows in halves:
            square = product(lefts[side, rows], rights[side])
            squares[side, rows] = square
            put_right(later, side, rows, *two_terms(square))
    for side in range(2):
        for rows in halves:
            cube = product(lefts[side, rows], later[side])
            matrix = stats[side, rows] * inverses[side]
            square = squares[side, rows]
            outer[side, rows] = (POLY[4] * matrix + POLY[5] * square + POLY[6] * cube).astype(BF16)
            cubes[side, rows] = cube.astype(BF16)
            row = lax.broadcasted_iota(jnp.int32, (ORDER // 2, ORDER), 0) + rows.start
            col = lax.broadcasted_iota(jnp.int32, (ORDER // 2, ORDER), 1)
            value = POLY[1] * matrix + POLY[2] * square + POLY[3] * cube
            squares[side, rows] = value + jnp.where(row == col, POLY[0], 0.0)
    for side in range(2):
        scale = lax.rsqrt(jnp.sqrt(norms[side]))
        for rows in halves:
            value = squares[side, rows] + product(cubes[side, rows], outer[side])
            roots[side, rows] = (value * scale).astype(BF16)
    for rows in halves:
        inner[rows] = product(grad[rows], roots[1]).astype(BF16)
    for rows in halves:
        result[rows] = product(roots[0, rows], inner[...])
    square = sum_of_squares([result[rows] for rows in halves])
    scale = jnp.sqrt(adam_sq) / (jnp.sqrt(square) + 1e-06)
    kept[...] = (result[:, pl.ds(pl.multiple_of(member * COLS, COLS), COLS)] * scale).astype(BF16)
    passed[...] = (result[:, pl.ds(pl.multiple_of((NARROW - 1 - member) * COLS, COLS), COLS)] * scale).astype(BF16)


def place_kernel(table, member_ref, arrived, update, wide, blocks):
    wide[...] = arrived[...].astype(F32).reshape(2, OWNERS // 2, 8, COLS)
    flip = member_ref[0] >> 1

    def eight_owners(step, carry):
        for k in range(8):
            for slot in range(2):
                block = table[(2 + slot) * OWNERS + step * 8 + k]
                first_row = ROWS * (k % 2)
                blocks[block] = wide[slot ^ flip, step * 4 + k // 2, first_row : first_row + ROWS]
        return carry

    lax.fori_loop(0, OWNERS // 8, eight_owners, 0)
    update[...] = blocks[0:BLOCKS].reshape(BLOCKS * ROWS, COLS).astype(BF16)


def call(kernel, in_specs, outs, scratch, vmem_mib, flops, moved):
    specs, shapes = zip(*outs)
    return pl.pallas_call(
        kernel,
        in_specs=in_specs,
        out_specs=list(specs),
        out_shape=[jax.ShapeDtypeStruct(*shape) for shape in shapes],
        scratch_shapes=scratch,
        compiler_params=pltpu.CompilerParams(vmem_limit_bytes=vmem_mib * 1024 * 1024),
        cost_estimate=pl.CostEstimate(flops=flops, bytes_accessed=moved, transcendentals=0),
    )


def per_device(grad_parts, first_moment, second_moment, factors, block_order, owner_counts):
    member = lax.axis_index("narrow").astype(jnp.int32).reshape(1)
    flat = BLOCKS * ROWS

    (partial_cols,) = call(
        columns_kernel,
        [ANY],
        [(VMEM, ((NARROW, BLOCKS, ROWS, COLS), BF16))],
        [pltpu.SemaphoreType.DMA((NARROW,))],
        16,
        0,
        1_600_000,
    )(grad_parts[0])
    partial_cols, block_order, owner_counts = lax.optimization_barrier((partial_cols, block_order, owner_counts))
    (table,) = call(table_kernel, [SMEM, SMEM], [(SMEM, ((4 * OWNERS,), jnp.int32))], [], 16, 0, 8_000_000)(
        block_order, owner_counts
    )
    partial_cols = lax.all_to_all(partial_cols, "narrow", 0, 0, tiled=True)

    factor, partial_cols = lax.optimization_barrier((factors[0, 0], partial_cols))
    other_factor = lax.ppermute(factor.astype(BF16), "narrow", [(0, 1), (1, 0), (2, 3), (3, 2)])

    new_first, new_second, outgoing = call(
        moments_kernel,
        [SMEM, VMEM, VMEM, VMEM],
        [(ANY, ((flat, COLS), F32)), (ANY, ((flat, COLS), F32)), (VMEM, ((OWNERS * GROUP, COLS), BF16))],
        [
            pltpu.VMEM((BLOCKS + 1, 16, COLS), F32),
            pltpu.VMEM((OWNERS * GROUP, COLS), F32),
            pltpu.VMEM((flat, COLS), F32),
            pltpu.VMEM((flat, COLS), F32),
            pltpu.SemaphoreType.DMA((2,)),
        ],
        16,
        4_000_000,
        2_800_000,
    )(
        table,
        partial_cols.reshape(NARROW, flat, COLS),
        first_moment.reshape(flat, COLS),
        second_moment.reshape(flat, COLS),
    )

    arrived = lax.all_to_all(outgoing.reshape(OWNERS, GROUP // 2, 2, COLS), "dp", 0, 0, tiled=True)
    (spread,) = call(
        spread_kernel,
        [VMEM],
        [(VMEM, ((NARROW, ORDER + 16, COLS), BF16))],
        [],
        16,
        1_000_000,
        900_000,
    )(arrived.reshape(OWNERS * GROUP, COLS))
    chunks = lax.all_to_all(spread, "narrow", 0, 0, tiled=True)

    square = (ORDER, ORDER)
    new_factor, kept, passed = call(
        owner_kernel,
        [SMEM, VMEM, VMEM, VMEM],
        [(VMEM, (square, F32)), (VMEM, ((ORDER, COLS), BF16)), (VMEM, ((ORDER, COLS), BF16))],
        [
            pltpu.VMEM(square, BF16),
            pltpu.VMEM((2, *square), F32),
            pltpu.VMEM((2, ORDER, 3 * ORDER), BF16),
            pltpu.VMEM((2, 3 * ORDER, ORDER), BF16),
            pltpu.VMEM((2, 3 * ORDER, ORDER), BF16),
            pltpu.VMEM((2, *square), F32),
            pltpu.VMEM((2, *square), BF16),
            pltpu.VMEM((2, *square), BF16),
            pltpu.VMEM((2, *square), BF16),
            pltpu.VMEM(square, BF16),
            pltpu.VMEM(square, F32),
        ],
        27,
        5_000_000_000,
        4_000_000,
    )(member, chunks, factor, other_factor)

    received = lax.ppermute(passed, "narrow", [(0, 3), (3, 0), (1, 2), (2, 1)])
    outgoing = jnp.stack([kept, received]).reshape(2, OWNERS, ROWS, COLS)
    came_back = lax.all_to_all(outgoing, "dp", 1, 1, tiled=True)
    (update,) = call(
        place_kernel,
        [SMEM, SMEM, VMEM],
        [(VMEM, ((flat, COLS), BF16))],
        [pltpu.VMEM((2, OWNERS // 2, 8, COLS), F32), pltpu.VMEM((BLOCKS + 8, ROWS, COLS), F32)],
        16,
        1_000_000,
        500_000,
    )(table, member, came_back.reshape(2, ORDER, COLS))
    local = (BLOCKS, ROWS, COLS)
    return update.reshape(local), new_first.reshape(local), new_second.reshape(local), new_factor[None, None]


def solution(mesh):
    return jax.shard_map(
        per_device,
        mesh=mesh,
        in_specs=(
            P("narrow", None, "dp", None),
            P(None, "dp", "narrow"),
            P(None, "dp", "narrow"),
            P("dp", "narrow", None, None),
            P(),
            P(),
        ),
        out_specs=(
            P(None, "dp", "narrow"),
            P(None, "dp", "narrow"),
            P(None, "dp", "narrow"),
            P("dp", "narrow", None, None),
        ),
        check_vma=False,
    )
```

time: 136 us -> 128 us (0.941)
  blocking collectives: 48.7 us -> 32.4 us
  waiting for transfers between devices: 34.9 us -> 40.7 us
  starting transfers between devices: 32.2 us -> 37.5 us
  local copies, waits for them, and re-layouts: 2.93 us -> 1.25 us
    all_to_all x1 -> x0, blocking collectives: 13.3 us -> none  [per_device(): partial_cols = lax.all_to_all(partial_cols, 'narrow', 0, 0, tiled=True)]
    all_to_all x0 -> x1, waiting for transfers between devices: none -> 5.95 us  [per_device(): partial_cols = lax.all_to_all(partial_cols, 'narrow', 0, 0, tiled=True)]
    all_to_all x0 -> x1, starting transfers between devices: none -> 5.16 us  [per_device(): partial_cols = lax.all_to_all(partial_cols, 'narrow', 0, 0, tiled=True)]
    all_to_all x1, blocking collectives: 35.5 us -> 32.4 us  [per_device(): came_back = lax.all_to_all(outgoing, 'dp', 1, 1, tiled=True)]
    another operation x2 -> x0, local copies, waits for them, and re-layouts: 2.15 us -> none  [per_device(): grad_parts[0].reshape(BLOCKS, ROWS, NARROW, COLS).transpose(2, 0, 1, 3)]
    pallas_call x4 -> x6, Pallas kernels: 15.6 us -> 15.1 us  [the longest x1 6.26 us: per_device(): call(owner_kernel, [SMEM, VMEM, VMEM, VMEM], [(VMEM, (square, F32)), (VME...]
  transfers between devices with their start and end apart: 4 -> 5, of which waited for: 3 -> 4; matrix products, arithmetic and copies ran while one was open for 0% -> 0% of each run, Pallas kernels for 1% -> 3%
where the time goes in v2:
time: 128 us
  waiting for transfers between devices  40.7 us (32%)
  starting transfers between devices  37.5 us (29%)
  blocking collectives  32.4 us (25%)
  Pallas kernels  15.1 us (12%)
    all_to_all x1, blocking collectives, per_device(): came_back = lax.all_to_all(outgoing, 'dp', 1, 1, tiled=True)  32.4 us
    all_to_all x1, starting transfers between devices, per_device(): lax.all_to_all(outgoing.reshape(OWNERS, GROUP // 2, 2, COLS), 'dp', 0, 0,...  23.8 us
    all_to_all x1, waiting for transfers between devices, per_device(): lax.all_to_all(outgoing.reshape(OWNERS, GROUP // 2, 2, COLS), 'dp', 0, 0,...  23.1 us
    all_to_all x1, waiting for transfers between devices, per_device(): chunks = lax.all_to_all(spread, 'narrow', 0, 0, tiled=True)  7.53 us
    pallas_call x1, Pallas kernels, per_device(): call(owner_kernel, [SMEM, VMEM, VMEM, VMEM], [(VMEM, (square, F32)), (VME...  6.26 us
    all_to_all x1, waiting for transfers between devices, per_device(): partial_cols = lax.all_to_all(partial_cols, 'narrow', 0, 0, tiled=True)  5.95 us
    all_to_all x1, starting transfers between devices, per_device(): partial_cols = lax.all_to_all(partial_cols, 'narrow', 0, 0, tiled=True)  5.16 us
    ppermute x1, waiting for transfers between devices, per_device(): received = lax.ppermute(passed, 'narrow', [(0, 3), (3, 0), (1, 2), (2, 1)])  4.07 us
  transfers between devices with their start and end apart: 5, of which 4 were waited for; matrix products, arithmetic and copies ran while one was open for 0% of the time, Pallas kernels for 3%

profile of v2, /device:TPU:1, one launch (start us, length us, event | category | flops | bytes accessed | tf_op | source)
XLA Modules:
  0.0 127.9 jit_solution(13867014861418605483)
XLA Ops:
  0.6 0.0 copy-start.1
  0.6 1.1 copy-done.1
  1.8 1.2 shard_map.93
  3.0 0.0 copy-start.4
  3.0 0.0 copy-start.5
  3.0 0.0 copy-start.2
  3.0 0.0 copy-start.3
  3.0 5.2 %all-to-all-start = ((bf16[4,192,4,128]{3,2,1,0:T(4,128)(2,1)}), bf16[4,192,4,128]{3,2,1,0:T(4,128)(2,1)S(1)}, u32[]{:S(2)}, u32[]{:S(2)}) async-start(bf16[4,192,4,128]{3,2,1,0:T(4,128)(2,1)} %shard_map.93), calls=%async_computation | async-start | bytes 1572864 | tf_op jit(solution)/shard_map/all_to_all | solution.py:263
  8.2 0.0 copy-done.4
  8.2 0.0 copy-done.5
  8.2 2.4 %shard_map.94.table = s32[512]{0:T(512)S(1)} custom-call(s32[192]{0:T(256)S(1)} %copy-done.4, s32[128]{0:T(128)S(1)} %copy-done.5), custom_call_target="tpu_custom_call" | custom-call | bytes 8000000 | tf_op jit(solution)/shard_map/pallas_call | solution.py:260
  10.6 6.0 %all-to-all-done = bf16[4,192,4,128]{3,2,1,0:T(4,128)(2,1)S(1)} async-done(((bf16[4,192,4,128]{3,2,1,0:T(4,128)(2,1)}), bf16[4,192,4,128]{3,2,1,0:T(4,128)(2,1)S(1)}, u32[]{:S(2)}, u32[]{:S(2)}) %all-to-all-start) | async-done | bytes 786464 | tf_op jit(solution)/shard_map/all_to_all | solution.py:263
  16.5 0.0 copy-done.2
  16.5 0.0 copy-done.3
  16.5 0.0 copy-start
  16.5 2.6 %shard_map.95 = (f32[768,128]{1,0:T(8,128)}, f32[768,128]{1,0:T(8,128)}, bf16[1280,128]{1,0:T(8,128)(2,1)}) custom-call(s32[512]{0:T(512)S(1)} %shard_map.94.table, bf16[4,768,128]{2,1,0:T(8,128)(2,1)S(1)} %bitcast.19, f32[768,128]{1,0:T(8,128)S(1)} %bitcast.25, f32[768,128]{1,0:T(8,128)S(1)} %bitcast.26), custom_call_target="tpu_custom_call" | custom-call | flops 4000000 | bytes 2800000 | tf_op jit(solution)/shard_map/pallas_call | solution.py:268
  19.1 23.8 %all-to-all-start.1 = ((bf16[128,5,2,128]{3,2,1,0:T(2,128)(2,1)}), bf16[128,5,2,128]{3,2,1,0:T(2,128)(2,1)S(1)}, u32[]{:S(2)}, u32[]{:S(2)}) async-start(bf16[128,5,2,128]{3,2,1,0:T(2,128)(2,1)} %bitcast.6), calls=%async_computation.1 | async-start | bytes 655360 | tf_op jit(solution)/shard_map/all_to_all | solution.py:289
  42.9 0.0 copy-done
  42.9 0.1 convert_element_type.3
  43.0 2.2 %collective-permute-start = (bf16[512,512]{1,0:T(8,128)(2,1)S(1)}, bf16[512,512]{1,0:T(8,128)(2,1)S(1)}, u32[]{:S(2)}, u32[]{:S(2)}) collective-permute-start(bf16[512,512]{1,0:T(8,128)(2,1)S(1)} %convert_element_type.3), channel_id=1, source_target_pairs={{0,1},{1,0},{2,3},{3,2},{4,5},{5,4},{6,7},{7,6},{8,9},{9,8},{10,11... | collective-permute-start | bytes 1572872 | tf_op jit(solution)/shard_map/ppermute | solution.py:266
  45.2 23.1 %all-to-all-done.1 = bf16[128,5,2,128]{3,2,1,0:T(2,128)(2,1)S(1)} async-done(((bf16[128,5,2,128]{3,2,1,0:T(2,128)(2,1)}), bf16[128,5,2,128]{3,2,1,0:T(2,128)(2,1)S(1)}, u32[]{:S(2)}, u32[]{:S(2)}) %all-to-all-start.1) | async-done | bytes 327712 | tf_op jit(solution)/shard_map/all_to_all | solution.py:289
  68.3 1.0 shard_map.96
  69.3 3.5 %all-to-all-start.2 = ((bf16[4,528,128]{2,1,0:T(8,128)(2,1)}), bf16[4,528,128]{2,1,0:T(8,128)(2,1)S(1)}, u32[]{:S(2)}, u32[]{:S(2)}) async-start(bf16[4,528,128]{2,1,0:T(8,128)(2,1)} %shard_map.96), calls=%async_computation.2 | async-start | bytes 1081344 | tf_op jit(solution)/shard_map/all_to_all | solution.py:299
  72.8 0.0 collective-permute-done.other
  72.8 7.5 %all-to-all-done.2.chunks = bf16[4,528,128]{2,1,0:T(8,128)(2,1)S(1)} async-done(((bf16[4,528,128]{2,1,0:T(8,128)(2,1)}), bf16[4,528,128]{2,1,0:T(8,128)(2,1)S(1)}, u32[]{:S(2)}, u32[]{:S(2)}) %all-to-all-start.2) | async-done | bytes 540704 | tf_op jit(solution)/shard_map/all_to_all | solution.py:299
  80.4 6.3 %shard_map.97 = (f32[512,512]{1,0:T(8,128)}, bf16[512,128]{1,0:T(8,128)(2,1)S(1)}, bf16[512,128]{1,0:T(8,128)(2,1)S(1)}) custom-call(s32[1]{0:T(128)} %bitcast.1.member_ref, bf16[4,528,128]{2,1,0:T(8,128)(2,1)S(1)} %all-to-all-done.2.chunks, f32[512,512]{1,0:T(8,128)S(1)} %bitcast.22, bf16[512,512]{1,0:T(8,128)(2,1)S(1)} %collective-permute-done.other), custom_call_target="tpu_custom_call" | custom-call | flops 5000000000 | bytes 4000000 | tf_op jit(solution)/shard_map/pallas_call | solution.py:302
  86.6 2.8 %collective-permute-start.1 = (bf16[512,128]{1,0:T(8,128)(2,1)S(1)}, bf16[512,128]{1,0:T(8,128)(2,1)S(1)}, u32[]{:S(2)}, u32[]{:S(2)}) collective-permute-start(bf16[512,128]{1,0:T(8,128)(2,1)S(1)} %get-tuple-element.22), channel_id=1, source_target_pairs={{0,3},{3,0},{1,2},{2,1},{4,7},{7,4},{5,6},{6,5},{8,11},{11,8},{9,1... | collective-permute-start | bytes 393224 | tf_op jit(solution)/shard_map/ppermute | solution.py:324
  89.5 4.1 %collective-permute-done.1 = bf16[512,128]{1,0:T(8,128)(2,1)S(1)} collective-permute-done((bf16[512,128]{1,0:T(8,128)(2,1)S(1)}, bf16[512,128]{1,0:T(8,128)(2,1)S(1)}, u32[]{:S(2)}, u32[]{:S(2)}) %collective-permute-start.1) | collective-permute-done | bytes 131104 | tf_op jit(solution)/shard_map/ppermute | solution.py:324
  93.5 0.2 pad_maximum_fusion
  93.7 32.4 %all_to_all.20 = bf16[2,128,4,128]{3,2,0,1:T(4,128)(2,1)S(1)} all-to-all(bf16[2,128,4,128]{3,2,0,1:T(4,128)(2,1)S(1)} %pad_maximum_fusion), channel_id=1, replica_groups=mesh['dp'=128,'narrow'=4] {'dp'}, dimensions={1} | all-to-all | bytes 524288 | tf_op jit(solution)/shard_map/all_to_all | solution.py:326
  126.1 0.1 copy.12
  126.2 1.7 %shard_map.98 = bf16[768,128]{1,0:T(8,128)(2,1)} custom-call(s32[512]{0:T(512)S(1)} %shard_map.94.table, s32[1]{0:T(128)} %bitcast.1.member_ref, bf16[2,512,128]{2,1,0:T(8,128)(2,1)S(1)} %bitcast.23), custom_call_target="tpu_custom_call" | custom-call | flops 1000000 | bytes 500000 | tf_op jit(solution)/shard_map/pallas_call | solution.py:327
Async XLA Ops:
  0.6 1.1 copy-start.1
  3.0 5.2 %copy-start.4 = (s32[192]{0:T(256)S(1)}, s32[192]{0:T(256)}, u32[]{:S(2)}) copy-start(s32[192]{0:T(256)} %order) | copy-start | bytes 2308
  3.0 5.2 %copy-start.5 = (s32[128]{0:T(128)S(1)}, s32[128]{0:T(128)}, u32[]{:S(2)}) copy-start(s32[128]{0:T(128)} %counts) | copy-start | bytes 1540
  3.0 13.5 %copy-start.2 = (f32[192,4,128]{2,1,0:T(4,128)S(1)}, f32[192,4,128]{2,1,0:T(4,128)}, u32[]{:S(2)}) copy-start(f32[192,4,128]{2,1,0:T(4,128)} %param.7) | copy-start | bytes 1179652
  3.0 13.5 %copy-start.3 = (f32[192,4,128]{2,1,0:T(4,128)S(1)}, f32[192,4,128]{2,1,0:T(4,128)}, u32[]{:S(2)}) copy-start(f32[192,4,128]{2,1,0:T(4,128)} %param.8) | copy-start | bytes 1179652
  3.0 13.5 %all-to-all-start = ((bf16[4,192,4,128]{3,2,1,0:T(4,128)(2,1)}), bf16[4,192,4,128]{3,2,1,0:T(4,128)(2,1)S(1)}, u32[]{:S(2)}, u32[]{:S(2)}) async-start(bf16[4,192,4,128]{3,2,1,0:T(4,128)(2,1)} %shard_map.93), calls=%async_computation | async-start | bytes 1572864 | tf_op jit(solution)/shard_map/all_to_all | solution.py:263
  16.5 26.4 %copy-start = (f32[1,1,512,512]{3,2,1,0:T(8,128)S(1)}, f32[1,1,512,512]{3,2,1,0:T(8,128)}, u32[]{:S(2)}) copy-start(f32[1,1,512,512]{3,2,1,0:T(8,128)} %param.9) | copy-start | bytes 3145732
  19.1 49.2 %all-to-all-start.1 = ((bf16[128,5,2,128]{3,2,1,0:T(2,128)(2,1)}), bf16[128,5,2,128]{3,2,1,0:T(2,128)(2,1)S(1)}, u32[]{:S(2)}, u32[]{:S(2)}) async-start(bf16[128,5,2,128]{3,2,1,0:T(2,128)(2,1)} %bitcast.6), calls=%async_computation.1 | async-start | bytes 655360 | tf_op jit(solution)/shard_map/all_to_all | solution.py:289
  43.0 29.8 %collective-permute-start = (bf16[512,512]{1,0:T(8,128)(2,1)S(1)}, bf16[512,512]{1,0:T(8,128)(2,1)S(1)}, u32[]{:S(2)}, u32[]{:S(2)}) collective-permute-start(bf16[512,512]{1,0:T(8,128)(2,1)S(1)} %convert_element_type.3), channel_id=1, source_target_pairs={{0,1},{1,0},{2,3},{3,2},{4,5},{5,4},{6,7},{7,6},{8,9},{9,8},{10,11... | collective-permute-start | bytes 1572872 | tf_op jit(solution)/shard_map/ppermute | solution.py:266
  69.3 11.0 %all-to-all-start.2 = ((bf16[4,528,128]{2,1,0:T(8,128)(2,1)}), bf16[4,528,128]{2,1,0:T(8,128)(2,1)S(1)}, u32[]{:S(2)}, u32[]{:S(2)}) async-start(bf16[4,528,128]{2,1,0:T(8,128)(2,1)} %shard_map.96), calls=%async_computation.2 | async-start | bytes 1081344 | tf_op jit(solution)/shard_map/all_to_all | solution.py:299
  86.6 6.9 %collective-permute-start.1 = (bf16[512,128]{1,0:T(8,128)(2,1)S(1)}, bf16[512,128]{1,0:T(8,128)(2,1)S(1)}, u32[]{:S(2)}, u32[]{:S(2)}) collective-permute-start(bf16[512,128]{1,0:T(8,128)(2,1)S(1)} %get-tuple-element.22), channel_id=1, source_target_pairs={{0,3},{3,0},{1,2},{2,1},{4,7},{7,4},{5,6},{6,5},{8,11},{11,8},{9,1... | collective-permute-start | bytes 393224 | tf_op jit(solution)/shard_map/ppermute | solution.py:324

commit v3 on v2

--- a/solution.py
+++ b/solution.py
@@ -3,7 +3,7 @@
 from jax import lax
 from jax.experimental import pallas as pl
 from jax.experimental.pallas import tpu as pltpu
-from jax.sharding import PartitionSpec as P
+from jax.sharding import Mesh, PartitionSpec as P
 
 BLOCKS = 192
 OWNERS = 128
@@ -11,7 +11,10 @@
 ROWS = 4
 COLS = 128
 ORDER = 512
-GROUP = 10
+CORES = 2
+CHIPS = OWNERS // CORES
+GROUP = 18
+HALF = CHIPS * ROWS
 BF16 = jnp.bfloat16
 F32 = jnp.float32
 VMEM = pl.BlockSpec(memory_space=pltpu.VMEM)
@@ -77,10 +80,11 @@
     entries[PAIRS : 2 * PAIRS, 4:8] = gradient[:, 0:4]
     squares = (adam * adam).reshape(PAIRS, 8, COLS)
     upper = lax.broadcasted_iota(jnp.int32, (1, 8, COLS), 1) < ROWS
-    fore = lax.broadcasted_iota(jnp.int32, (1, 8, COLS), 2) < 3
+    wide_lane = lax.broadcasted_iota(jnp.int32, (1, 8, COLS), 2)
+    fore = (wide_lane < 3) | ((wide_lane >= 6) & (wide_lane < 9))
     row_sums = jnp.sum(squares, axis=2, keepdims=True)
     lane = lax.broadcasted_iota(jnp.int32, (1, 1, COLS), 2)
-    term = jnp.where(lane >= 3, lane - 3, lane)
+    term = sum(jnp.where(lane >= at, -3, 0) for at in (3, 6, 9)) + lane
     for half in range(2):
         pick = (upper == fore) if half == 0 else (upper != fore)
         total = jnp.sum(jnp.where(pick, row_sums, 0.0), axis=1, keepdims=True)
@@ -91,38 +95,46 @@
     row = lax.broadcasted_iota(jnp.int32, (8, COLS), 0)
     across = lax.broadcasted_iota(jnp.int32, (1, COLS), 1)
 
-    def four_owners(step, carry):
+    def four_chips(step, carry):
         base = pl.multiple_of(step * (4 * GROUP), 8)
         for k in range(4):
-            entry0 = table[step * 4 + k]
-            entry1 = table[OWNERS + step * 4 + k]
-            slots[pl.ds(base + GROUP * k, 8)] = jnp.where(row < ROWS, entries[entry0, 0:8], entries[entry1, 0:8])
-            totals = jnp.where(across < 3, entries[entry0, 8:9], entries[entry1, 8:9])
-            slots[pl.ds(base + GROUP * k + 8, 2)] = jnp.broadcast_to(totals, (2, COLS))
+            at = base + GROUP * k
+            totals = []
+            for core in range(CORES):
+                owner = (step * 4 + k) * CORES + core
+                entry0, entry1 = table[owner], table[OWNERS + owner]
+                slots[pl.ds(at + 8 * core, 8)] = jnp.where(row < ROWS, entries[entry0, 0:8], entries[entry1, 0:8])
+                totals += [entries[entry0, 8:9], entries[entry1, 8:9]]
+            first_owner = jnp.where(across < 3, totals[0], totals[1])
+            second_owner = jnp.where(across < 9, totals[2], totals[3])
+            totals = jnp.where(across < 6, first_owner, second_owner)
+            slots[pl.ds(at + 16, 2)] = jnp.broadcast_to(totals, (2, COLS))
         return carry
 
-    lax.fori_loop(0, OWNERS // 4, four_owners, 0)
+    lax.fori_loop(0, CHIPS // 4, four_chips, 0)
     out[...] = slots[...].astype(BF16)
     for copy in copies:
         copy.wait()
 
 
 def spread_kernel(arrived, out):
-    groups = arrived[...].astype(F32).reshape(OWNERS // 4, 4 * GROUP, COLS)
+    groups = arrived[...].astype(F32).reshape(CHIPS // 4, 4 * GROUP, COLS)
     starts = [GROUP * k for k in range(4)]
-    total = jnp.sum(sum(groups[:, at + 8 : at + 9] for at in starts), axis=0)
+    total = jnp.sum(sum(groups[:, at + 16 : at + 17] for at in starts), axis=0)
     across = lax.broadcasted_iota(jnp.int32, (1, COLS), 1)
-    for slot in range(2):
-        rows = [groups[:, at + ROWS * slot : at + ROWS * (slot + 1)] for at in starts]
-        block = jnp.concatenate(rows, axis=1).reshape(ORDER, COLS).astype(BF16)
-        mine = (across >= 3 * slot) & (across < 3 * slot + 3)
-        sum_sq = jnp.sum(jnp.where(mine, total, 0.0), axis=1, keepdims=True)
-        high, middle, low = three_terms(jnp.broadcast_to(sum_sq, (1, COLS)))
-        pieces = jnp.where(across == 0, high, jnp.where(across == 1, middle, jnp.where(across == 2, low, 0.0)))
-        pieces = jnp.broadcast_to(pieces, (16, COLS)).astype(BF16)
-        for member in (2 * slot, 2 * slot + 1):
-            out[member, 0:ORDER] = block
-            out[member, ORDER : ORDER + 16] = pieces
+    for core in range(CORES):
+        for slot in range(2):
+            place = 2 * core + slot
+            rows = [groups[:, at + ROWS * place : at + ROWS * (place + 1)] for at in starts]
+            block = jnp.concatenate(rows, axis=1).reshape(HALF, COLS).astype(BF16)
+            mine = (across >= 3 * place) & (across < 3 * place + 3)
+            sum_sq = jnp.sum(jnp.where(mine, total, 0.0), axis=1, keepdims=True)
+            high, middle, low = three_terms(jnp.broadcast_to(sum_sq, (1, COLS)))
+            pieces = jnp.where(across == 0, high, jnp.where(across == 1, middle, jnp.where(across == 2, low, 0.0)))
+            pieces = jnp.broadcast_to(pieces, (16, COLS)).astype(BF16)
+            for member in (2 * slot, 2 * slot + 1):
+                out[NARROW * core + member, 0:HALF] = block
+                out[NARROW * core + member, HALF : HALF + 16] = pieces
 
 
 def product(left, right, contract=((1,), (0,))):
@@ -146,8 +158,9 @@
     is_right = (member & 1) == 1
     halves = [slice(0, ORDER // 2), slice(ORDER // 2, ORDER)]
     for n in range(NARROW):
-        grad[:, COLS * n : COLS * (n + 1)] = chunks[n, 0:ORDER]
-    adam_sq = sum(chunks[n, ORDER : ORDER + 16].astype(F32)[0:1] for n in range(NARROW))
+        rows = [chunks[NARROW * core + n, 0:HALF].astype(F32).reshape(CHIPS, ROWS, COLS) for core in range(CORES)]
+        grad[:, COLS * n : COLS * (n + 1)] = jnp.concatenate(rows, axis=1).reshape(ORDER, COLS).astype(BF16)
+    adam_sq = sum(chunks[k, HALF : HALF + 16].astype(F32)[0:1] for k in range(CORES * NARROW))
     adam_sq = jnp.sum(adam_sq, axis=1, keepdims=True)
 
     def statistics(left_factor, right_factor, side):
@@ -268,10 +281,10 @@
     new_first, new_second, outgoing = call(
         moments_kernel,
         [SMEM, VMEM, VMEM, VMEM],
-        [(ANY, ((flat, COLS), F32)), (ANY, ((flat, COLS), F32)), (VMEM, ((OWNERS * GROUP, COLS), BF16))],
+        [(ANY, ((flat, COLS), F32)), (ANY, ((flat, COLS), F32)), (VMEM, ((CHIPS * GROUP, COLS), BF16))],
         [
             pltpu.VMEM((BLOCKS + 1, 16, COLS), F32),
-            pltpu.VMEM((OWNERS * GROUP, COLS), F32),
+            pltpu.VMEM((CHIPS * GROUP, COLS), F32),
             pltpu.VMEM((flat, COLS), F32),
             pltpu.VMEM((flat, COLS), F32),
             pltpu.SemaphoreType.DMA((2,)),
@@ -286,17 +299,17 @@
         second_moment.reshape(flat, COLS),
     )
 
-    arrived = lax.all_to_all(outgoing.reshape(OWNERS, GROUP // 2, 2, COLS), "dp", 0, 0, tiled=True)
+    arrived = lax.all_to_all(outgoing.reshape(CHIPS, GROUP // 2, 2, COLS), "chip", 0, 0, tiled=True)
     (spread,) = call(
         spread_kernel,
         [VMEM],
-        [(VMEM, ((NARROW, ORDER + 16, COLS), BF16))],
+        [(VMEM, ((CORES * NARROW, HALF + 16, COLS), BF16))],
         [],
         16,
         1_000_000,
         900_000,
-    )(arrived.reshape(OWNERS * GROUP, COLS))
-    chunks = lax.all_to_all(spread, "narrow", 0, 0, tiled=True)
+    )(arrived.reshape(CHIPS * GROUP, COLS))
+    chunks = lax.all_to_all(spread, ("core", "narrow"), 0, 0, tiled=True)
 
     square = (ORDER, ORDER)
     new_factor, kept, passed = call(
@@ -323,7 +336,7 @@
 
     received = lax.ppermute(passed, "narrow", [(0, 3), (3, 0), (1, 2), (2, 1)])
     outgoing = jnp.stack([kept, received]).reshape(2, OWNERS, ROWS, COLS)
-    came_back = lax.all_to_all(outgoing, "dp", 1, 1, tiled=True)
+    came_back = lax.all_to_all(outgoing, ("chip", "core"), 1, 1, tiled=True)
     (update,) = call(
         place_kernel,
         [SMEM, SMEM, VMEM],
@@ -338,22 +351,14 @@
 
 
 def solution(mesh):
+    devices = mesh.devices.reshape(CHIPS, CORES, NARROW)
+    rows = ("chip", "core")
+    moments = P(None, rows, "narrow")
+    factors = P(rows, "narrow", None, None)
     return jax.shard_map(
         per_device,
-        mesh=mesh,
-        in_specs=(
-            P("narrow", None, "dp", None),
-            P(None, "dp", "narrow"),
-            P(None, "dp", "narrow"),
-            P("dp", "narrow", None, None),
-            P(),
-            P(),
-        ),
-        out_specs=(
-            P(None, "dp", "narrow"),
-            P(None, "dp", "narrow"),
-            P(None, "dp", "narrow"),
-            P("dp", "narrow", None, None),
-        ),
+        mesh=Mesh(devices, ("chip", "core", "narrow")),
+        in_specs=(P("narrow", None, rows, None), moments, moments, factors, P(), P()),
+        out_specs=(moments, moments, moments, factors),
         check_vma=False,
     )

time: 128 us -> 125 us (0.977)
  waiting for transfers between devices: 40.7 us -> 37.4 us
  blocking collectives: 32.4 us -> 30.3 us
  starting transfers between devices: 37.5 us -> 39.3 us
    all_to_all x2, waiting for transfers between devices: 30.6 us -> 26.6 us  [the longest x1 16.8 us: per_device(): lax.all_to_all(outgoing.reshape(CHIPS, GROUP // 2, 2, COLS), 'chip', 0, 0...]
    all_to_all x1, blocking collectives: 32.4 us -> 30.3 us  [per_device(): came_back = lax.all_to_all(outgoing, ('chip', 'core'), 1, 1, tiled=True)]
    all_to_all x2, starting transfers between devices: 27.3 us -> 29 us  [the longest x1 21.3 us: per_device(): lax.all_to_all(outgoing.reshape(CHIPS, GROUP // 2, 2, COLS), 'chip', 0, 0...]
where the time goes in v3:
time: 125 us; the launch traced here: 124 us
  starting transfers between devices  39.3 us (31%)
  waiting for transfers between devices  37.4 us (30%)
  blocking collectives  30.3 us (24%)
  Pallas kernels  15.1 us (12%)
  local copies, waits for them, and re-layouts  1.25 us (1%)
    all_to_all x1, blocking collectives, per_device(): came_back = lax.all_to_all(outgoing, ('chip', 'core'), 1, 1, tiled=True)  30.3 us
    all_to_all x1, starting transfers between devices, per_device(): lax.all_to_all(outgoing.reshape(CHIPS, GROUP // 2, 2, COLS), 'chip', 0, 0...  21.3 us
    all_to_all x1, waiting for transfers between devices, per_device(): lax.all_to_all(outgoing.reshape(CHIPS, GROUP // 2, 2, COLS), 'chip', 0, 0...  16.8 us
    all_to_all x1, waiting for transfers between devices, per_device(): chunks = lax.all_to_all(spread, ('core', 'narrow'), 0, 0, tiled=True)  9.72 us
    all_to_all x1, starting transfers between devices, per_device(): chunks = lax.all_to_all(spread, ('core', 'narrow'), 0, 0, tiled=True)  7.63 us
    pallas_call x1, Pallas kernels, per_device(): call(owner_kernel, [SMEM, VMEM, VMEM, VMEM], [(VMEM, (square, F32)), (VME...  6.36 us
    all_to_all x1, waiting for transfers between devices, per_device(): partial_cols = lax.all_to_all(partial_cols, 'narrow', 0, 0, tiled=True)  5.95 us
    all_to_all x1, starting transfers between devices, per_device(): partial_cols = lax.all_to_all(partial_cols, 'narrow', 0, 0, tiled=True)  5.16 us
  transfers between devices with their start and end apart: 5, of which 4 were waited for; matrix products, arithmetic and copies ran while one was open for 0% of the time, Pallas kernels for 3%

profile of v3, /device:TPU:1, one launch (start us, length us, event | category | flops | bytes accessed | tf_op | source)
XLA Modules:
  0.0 124.4 jit_solution(5504453249468270803)
XLA Ops:
  0.6 0.0 copy-start.1
  0.6 1.1 copy-done.1
  1.8 1.2 shard_map.93
  3.0 0.0 copy-start.4
  3.0 0.0 copy-start.5
  3.0 0.0 copy-start.2
  3.0 0.0 copy-start.3
  3.0 5.2 %all-to-all-start = ((bf16[4,192,4,128]{3,2,1,0:T(4,128)(2,1)}), bf16[4,192,4,128]{3,2,1,0:T(4,128)(2,1)S(1)}, u32[]{:S(2)}, u32[]{:S(2)}) async-start(bf16[4,192,4,128]{3,2,1,0:T(4,128)(2,1)} %shard_map.93), calls=%async_computation | async-start | bytes 1572864 | tf_op jit(solution)/shard_map/all_to_all | solution.py:276
  8.2 0.0 copy-done.4
  8.2 0.0 copy-done.5
  8.2 2.4 %shard_map.94.table = s32[512]{0:T(512)S(1)} custom-call(s32[192]{0:T(256)S(1)} %copy-done.4, s32[128]{0:T(128)S(1)} %copy-done.5), custom_call_target="tpu_custom_call" | custom-call | bytes 8000000 | tf_op jit(solution)/shard_map/pallas_call | solution.py:273
  10.6 6.0 %all-to-all-done = bf16[4,192,4,128]{3,2,1,0:T(4,128)(2,1)S(1)} async-done(((bf16[4,192,4,128]{3,2,1,0:T(4,128)(2,1)}), bf16[4,192,4,128]{3,2,1,0:T(4,128)(2,1)S(1)}, u32[]{:S(2)}, u32[]{:S(2)}) %all-to-all-start) | async-done | bytes 786464 | tf_op jit(solution)/shard_map/all_to_all | solution.py:276
  16.5 0.0 copy-done.2
  16.5 0.0 copy-done.3
  16.5 0.0 copy-start
  16.5 2.6 %shard_map.95 = (f32[768,128]{1,0:T(8,128)}, f32[768,128]{1,0:T(8,128)}, bf16[1152,128]{1,0:T(8,128)(2,1)}) custom-call(s32[512]{0:T(512)S(1)} %shard_map.94.table, bf16[4,768,128]{2,1,0:T(8,128)(2,1)S(1)} %bitcast.19, f32[768,128]{1,0:T(8,128)S(1)} %bitcast.25, f32[768,128]{1,0:T(8,128)S(1)} %bitcast.26), custom_call_target="tpu_custom_call" | custom-call | flops 4000000 | bytes 2800000 | tf_op jit(solution)/shard_map/pallas_call | solution.py:281
  19.1 21.3 %all-to-all-start.1 = ((bf16[64,9,2,128]{3,2,1,0:T(2,128)(2,1)}), bf16[64,9,2,128]{3,2,1,0:T(2,128)(2,1)S(1)}, u32[]{:S(2)}, u32[]{:S(2)}) async-start(bf16[64,9,2,128]{3,2,1,0:T(2,128)(2,1)} %bitcast.6), calls=%async_computation.1 | async-start | bytes 589824 | tf_op jit(solution)/shard_map/all_to_all | solution.py:302
  40.5 0.0 copy-done
  40.5 0.1 convert_element_type.3
  40.5 2.2 %collective-permute-start = (bf16[512,512]{1,0:T(8,128)(2,1)S(1)}, bf16[512,512]{1,0:T(8,128)(2,1)S(1)}, u32[]{:S(2)}, u32[]{:S(2)}) collective-permute-start(bf16[512,512]{1,0:T(8,128)(2,1)S(1)} %convert_element_type.3), channel_id=1, source_target_pairs={{0,1},{1,0},{2,3},{3,2},{4,5},{5,4},{6,7},{7,6},{8,9},{9,8},{10,11... | collective-permute-start | bytes 1572872 | tf_op jit(solution)/shard_map/ppermute | solution.py:279
  42.7 16.8 %all-to-all-done.1 = bf16[64,9,2,128]{3,2,1,0:T(2,128)(2,1)S(1)} async-done(((bf16[64,9,2,128]{3,2,1,0:T(2,128)(2,1)}), bf16[64,9,2,128]{3,2,1,0:T(2,128)(2,1)S(1)}, u32[]{:S(2)}, u32[]{:S(2)}) %all-to-all-start.1) | async-done | bytes 294944 | tf_op jit(solution)/shard_map/all_to_all | solution.py:302
  59.6 0.9 shard_map.96
  60.5 7.6 %all-to-all-start.2 = ((bf16[8,272,128]{2,1,0:T(8,128)(2,1)}), bf16[8,272,128]{2,1,0:T(8,128)(2,1)S(1)}, u32[]{:S(2)}, u32[]{:S(2)}) async-start(bf16[8,272,128]{2,1,0:T(8,128)(2,1)} %shard_map.96), calls=%async_computation.2 | async-start | bytes 1114112 | tf_op jit(solution)/shard_map/all_to_all | solution.py:312
  68.2 0.0 collective-permute-done.other
  68.2 9.7 %all-to-all-done.2.chunks = bf16[8,272,128]{2,1,0:T(8,128)(2,1)S(1)} async-done(((bf16[8,272,128]{2,1,0:T(8,128)(2,1)}), bf16[8,272,128]{2,1,0:T(8,128)(2,1)S(1)}, u32[]{:S(2)}, u32[]{:S(2)}) %all-to-all-start.2) | async-done | bytes 557088 | tf_op jit(solution)/shard_map/all_to_all | solution.py:312
  77.9 6.4 %shard_map.97 = (f32[512,512]{1,0:T(8,128)}, bf16[512,128]{1,0:T(8,128)(2,1)S(1)}, bf16[512,128]{1,0:T(8,128)(2,1)S(1)}) custom-call(s32[1]{0:T(128)} %bitcast.1.member_ref, bf16[8,272,128]{2,1,0:T(8,128)(2,1)S(1)} %all-to-all-done.2.chunks, f32[512,512]{1,0:T(8,128)S(1)} %bitcast.22, bf16[512,512]{1,0:T(8,128)(2,1)S(1)} %collective-permute-done.other), custom_call_target="tpu_custom_call" | custom-call | flops 5000000000 | bytes 4000000 | tf_op jit(solution)/shard_map/pallas_call | solution.py:315
  84.2 2.9 %collective-permute-start.1 = (bf16[512,128]{1,0:T(8,128)(2,1)S(1)}, bf16[512,128]{1,0:T(8,128)(2,1)S(1)}, u32[]{:S(2)}, u32[]{:S(2)}) collective-permute-start(bf16[512,128]{1,0:T(8,128)(2,1)S(1)} %get-tuple-element.22), channel_id=1, source_target_pairs={{0,3},{3,0},{1,2},{2,1},{4,7},{7,4},{5,6},{6,5},{8,11},{11,8},{9,1... | collective-permute-start | bytes 393224 | tf_op jit(solution)/shard_map/ppermute | solution.py:337
  87.2 4.9 %collective-permute-done.1 = bf16[512,128]{1,0:T(8,128)(2,1)S(1)} collective-permute-done((bf16[512,128]{1,0:T(8,128)(2,1)S(1)}, bf16[512,128]{1,0:T(8,128)(2,1)S(1)}, u32[]{:S(2)}, u32[]{:S(2)}) %collective-permute-start.1) | collective-permute-done | bytes 131104 | tf_op jit(solution)/shard_map/ppermute | solution.py:337
  92.1 0.2 pad_maximum_fusion
  92.3 30.3 %all_to_all.20 = bf16[2,128,4,128]{3,2,0,1:T(4,128)(2,1)S(1)} all-to-all(bf16[2,128,4,128]{3,2,0,1:T(4,128)(2,1)S(1)} %pad_maximum_fusion), channel_id=1, replica_groups=mesh['chip'=64,'core'=2,'narrow'=4] {'chip','core'}, dimensions={1} | all-to-all | bytes 524288 | tf_op jit(solution)/shard_map/all_to_all | solution.py:339
  122.6 0.1 copy.12
  122.7 1.7 %shard_map.98 = bf16[768,128]{1,0:T(8,128)(2,1)} custom-call(s32[512]{0:T(512)S(1)} %shard_map.94.table, s32[1]{0:T(128)} %bitcast.1.member_ref, bf16[2,512,128]{2,1,0:T(8,128)(2,1)S(1)} %bitcast.23), custom_call_target="tpu_custom_call" | custom-call | flops 1000000 | bytes 500000 | tf_op jit(solution)/shard_map/pallas_call | solution.py:340
Async XLA Ops:
  0.6 1.1 copy-start.1
  3.0 5.2 %copy-start.4 = (s32[192]{0:T(256)S(1)}, s32[192]{0:T(256)}, u32[]{:S(2)}) copy-start(s32[192]{0:T(256)} %order) | copy-start | bytes 2308
  3.0 5.2 %copy-start.5 = (s32[128]{0:T(128)S(1)}, s32[128]{0:T(128)}, u32[]{:S(2)}) copy-start(s32[128]{0:T(128)} %counts) | copy-start | bytes 1540
  3.0 13.5 %copy-start.2 = (f32[192,4,128]{2,1,0:T(4,128)S(1)}, f32[192,4,128]{2,1,0:T(4,128)}, u32[]{:S(2)}) copy-start(f32[192,4,128]{2,1,0:T(4,128)} %param.7) | copy-start | bytes 1179652
  3.0 13.5 %copy-start.3 = (f32[192,4,128]{2,1,0:T(4,128)S(1)}, f32[192,4,128]{2,1,0:T(4,128)}, u32[]{:S(2)}) copy-start(f32[192,4,128]{2,1,0:T(4,128)} %param.8) | copy-start | bytes 1179652
  3.0 13.5 %all-to-all-start = ((bf16[4,192,4,128]{3,2,1,0:T(4,128)(2,1)}), bf16[4,192,4,128]{3,2,1,0:T(4,128)(2,1)S(1)}, u32[]{:S(2)}, u32[]{:S(2)}) async-start(bf16[4,192,4,128]{3,2,1,0:T(4,128)(2,1)} %shard_map.93), calls=%async_computation | async-start | bytes 1572864 | tf_op jit(solution)/shard_map/all_to_all | solution.py:276
  16.5 23.9 %copy-start = (f32[1,1,512,512]{3,2,1,0:T(8,128)S(1)}, f32[1,1,512,512]{3,2,1,0:T(8,128)}, u32[]{:S(2)}) copy-start(f32[1,1,512,512]{3,2,1,0:T(8,128)} %param.9) | copy-start | bytes 3145732
  19.1 40.5 %all-to-all-start.1 = ((bf16[64,9,2,128]{3,2,1,0:T(2,128)(2,1)}), bf16[64,9,2,128]{3,2,1,0:T(2,128)(2,1)S(1)}, u32[]{:S(2)}, u32[]{:S(2)}) async-start(bf16[64,9,2,128]{3,2,1,0:T(2,128)(2,1)} %bitcast.6), calls=%async_computation.1 | async-start | bytes 589824 | tf_op jit(solution)/shard_map/all_to_all | solution.py:302
  40.5 27.6 %collective-permute-start = (bf16[512,512]{1,0:T(8,128)(2,1)S(1)}, bf16[512,512]{1,0:T(8,128)(2,1)S(1)}, u32[]{:S(2)}, u32[]{:S(2)}) collective-permute-start(bf16[512,512]{1,0:T(8,128)(2,1)S(1)} %convert_element_type.3), channel_id=1, source_target_pairs={{0,1},{1,0},{2,3},{3,2},{4,5},{5,4},{6,7},{7,6},{8,9},{9,8},{10,11... | collective-permute-start | bytes 1572872 | tf_op jit(solution)/shard_map/ppermute | solution.py:279
  60.5 17.4 %all-to-all-start.2 = ((bf16[8,272,128]{2,1,0:T(8,128)(2,1)}), bf16[8,272,128]{2,1,0:T(8,128)(2,1)S(1)}, u32[]{:S(2)}, u32[]{:S(2)}) async-start(bf16[8,272,128]{2,1,0:T(8,128)(2,1)} %shard_map.96), calls=%async_computation.2 | async-start | bytes 1114112 | tf_op jit(solution)/shard_map/all_to_all | solution.py:312
  84.2 7.8 %collective-permute-start.1 = (bf16[512,128]{1,0:T(8,128)(2,1)S(1)}, bf16[512,128]{1,0:T(8,128)(2,1)S(1)}, u32[]{:S(2)}, u32[]{:S(2)}) collective-permute-start(bf16[512,128]{1,0:T(8,128)(2,1)S(1)} %get-tuple-element.22), channel_id=1, source_target_pairs={{0,3},{3,0},{1,2},{2,1},{4,7},{7,4},{5,6},{6,5},{8,11},{11,8},{9,1... | collective-permute-start | bytes 393224 | tf_op jit(solution)/shard_map/ppermute | solution.py:337

commit v4 on v3

--- a/solution.py
+++ b/solution.py
@@ -152,10 +152,10 @@
 
 
 def owner_kernel(
-    member_ref, chunks, mine, other, new_mine, kept, passed, grad, stats, lefts, rights, later, squares, outer, cubes, roots, inner, result
+    place_ref, chunks, mine, other, new_mine, outgoing, grad, stats, lefts, rights, later, squares, outer, cubes, roots, inner, result
 ):
-    member = member_ref[0]
-    is_right = (member & 1) == 1
+    here, core = place_ref[0], place_ref[1]
+    is_right = here == 1
     halves = [slice(0, ORDER // 2), slice(ORDER // 2, ORDER)]
     for n in range(NARROW):
         rows = [chunks[NARROW * core + n, 0:HALF].astype(F32).reshape(CHIPS, ROWS, COLS) for core in range(CORES)]
@@ -223,23 +223,32 @@
         result[rows] = product(roots[0, rows], inner[...])
     square = sum_of_squares([result[rows] for rows in halves])
     scale = jnp.sqrt(adam_sq) / (jnp.sqrt(square) + 1e-06)
-    kept[...] = (result[:, pl.ds(pl.multiple_of(member * COLS, COLS), COLS)] * scale).astype(BF16)
-    passed[...] = (result[:, pl.ds(pl.multiple_of((NARROW - 1 - member) * COLS, COLS), COLS)] * scale).astype(BF16)
-
-
-def place_kernel(table, member_ref, arrived, update, wide, blocks):
-    wide[...] = arrived[...].astype(F32).reshape(2, OWNERS // 2, 8, COLS)
-    flip = member_ref[0] >> 1
-
-    def eight_owners(step, carry):
-        for k in range(8):
-            for slot in range(2):
-                block = table[(2 + slot) * OWNERS + step * 8 + k]
-                first_row = ROWS * (k % 2)
-                blocks[block] = wide[slot ^ flip, step * 4 + k // 2, first_row : first_row + ROWS]
+    for pair in range(2):
+        cols = result[:, pl.ds(pl.multiple_of((2 * pair + here) * COLS, COLS), COLS)] * scale
+        cols = cols.reshape(CHIPS, CORES * ROWS, COLS)
+        lower, upper = cols[:, 0:ROWS], cols[:, ROWS : 2 * ROWS]
+        staying = jnp.where(core == 0, lower, upper).reshape(HALF, COLS)
+        crossing = jnp.where(core == 0, upper, lower).reshape(HALF, COLS)
+        outgoing[0, pair * HALF : (pair + 1) * HALF] = staying.astype(BF16)
+        outgoing[1, pair * HALF : (pair + 1) * HALF] = crossing.astype(BF16)
+
+
+def place_kernel(table, place_ref, stayed, crossed, update, wide, blocks):
+    wide[0] = stayed[...].astype(F32).reshape(OWNERS // 2, 8, COLS)
+    wide[1] = crossed[...].astype(F32).reshape(OWNERS // 2, 8, COLS)
+    here = place_ref[1]
+
+    def four_chips(step, carry):
+        for k in range(4):
+            for core in range(CORES):
+                for slot in range(2):
+                    block = table[(2 + slot) * OWNERS + (step * 4 + k) * CORES + core]
+                    group = slot * (CHIPS // 2) + step * 2 + k // 2
+                    first_row = ROWS * (k % 2)
+                    blocks[block] = wide[core ^ here, group, first_row : first_row + ROWS]
         return carry
 
-    lax.fori_loop(0, OWNERS // 8, eight_owners, 0)
+    lax.fori_loop(0, CHIPS // 4, four_chips, 0)
     update[...] = blocks[0:BLOCKS].reshape(BLOCKS * ROWS, COLS).astype(BF16)
 
 
@@ -257,7 +266,7 @@
 
 
 def per_device(grad_parts, first_moment, second_moment, factors, block_order, owner_counts):
-    member = lax.axis_index("narrow").astype(jnp.int32).reshape(1)
+    place = jnp.stack([lax.axis_index("side"), lax.axis_index("core")]).astype(jnp.int32)
     flat = BLOCKS * ROWS
 
     (partial_cols,) = call(
@@ -273,10 +282,10 @@
     (table,) = call(table_kernel, [SMEM, SMEM], [(SMEM, ((4 * OWNERS,), jnp.int32))], [], 16, 0, 8_000_000)(
         block_order, owner_counts
     )
-    partial_cols = lax.all_to_all(partial_cols, "narrow", 0, 0, tiled=True)
+    partial_cols = lax.all_to_all(partial_cols, ("pair", "side"), 0, 0, tiled=True)
 
     factor, partial_cols = lax.optimization_barrier((factors[0, 0], partial_cols))
-    other_factor = lax.ppermute(factor.astype(BF16), "narrow", [(0, 1), (1, 0), (2, 3), (3, 2)])
+    other_factor = lax.ppermute(factor.astype(BF16), "side", [(0, 1), (1, 0)])
 
     new_first, new_second, outgoing = call(
         moments_kernel,
@@ -309,13 +318,13 @@
         1_000_000,
         900_000,
     )(arrived.reshape(CHIPS * GROUP, COLS))
-    chunks = lax.all_to_all(spread, ("core", "narrow"), 0, 0, tiled=True)
+    chunks = lax.all_to_all(spread, ("core", "pair", "side"), 0, 0, tiled=True)
 
     square = (ORDER, ORDER)
-    new_factor, kept, passed = call(
+    new_factor, outgoing = call(
         owner_kernel,
         [SMEM, VMEM, VMEM, VMEM],
-        [(VMEM, (square, F32)), (VMEM, ((ORDER, COLS), BF16)), (VMEM, ((ORDER, COLS), BF16))],
+        [(VMEM, (square, F32)), (VMEM, ((2, ORDER, COLS), BF16))],
         [
             pltpu.VMEM(square, BF16),
             pltpu.VMEM((2, *square), F32),
@@ -332,33 +341,33 @@
         27,
         5_000_000_000,
         4_000_000,
-    )(member, chunks, factor, other_factor)
-
-    received = lax.ppermute(passed, "narrow", [(0, 3), (3, 0), (1, 2), (2, 1)])
-    outgoing = jnp.stack([kept, received]).reshape(2, OWNERS, ROWS, COLS)
-    came_back = lax.all_to_all(outgoing, ("chip", "core"), 1, 1, tiled=True)
+    )(place, chunks, factor, other_factor)
+
+    came_back = lax.all_to_all(outgoing.reshape(2, OWNERS, ROWS, COLS), ("pair", "chip"), 1, 1, tiled=True)
+    came_back = came_back.reshape(2, ORDER, COLS)
+    crossed = lax.ppermute(came_back[1], "core", [(0, 1), (1, 0)])
     (update,) = call(
         place_kernel,
-        [SMEM, SMEM, VMEM],
+        [SMEM, SMEM, VMEM, VMEM],
         [(VMEM, ((flat, COLS), BF16))],
         [pltpu.VMEM((2, OWNERS // 2, 8, COLS), F32), pltpu.VMEM((BLOCKS + 8, ROWS, COLS), F32)],
         16,
         1_000_000,
         500_000,
-    )(table, member, came_back.reshape(2, ORDER, COLS))
+    )(table, place, came_back[0], crossed)
     local = (BLOCKS, ROWS, COLS)
     return update.reshape(local), new_first.reshape(local), new_second.reshape(local), new_factor[None, None]
 
 
 def solution(mesh):
-    devices = mesh.devices.reshape(CHIPS, CORES, NARROW)
-    rows = ("chip", "core")
-    moments = P(None, rows, "narrow")
-    factors = P(rows, "narrow", None, None)
+    devices = mesh.devices.reshape(CHIPS, CORES, NARROW // 2, 2)
+    rows, cols = ("chip", "core"), ("pair", "side")
+    moments = P(None, rows, cols)
+    factors = P(rows, cols, None, None)
     return jax.shard_map(
         per_device,
-        mesh=Mesh(devices, ("chip", "core", "narrow")),
-        in_specs=(P("narrow", None, rows, None), moments, moments, factors, P(), P()),
+        mesh=Mesh(devices, rows + cols),
+        in_specs=(P(cols, None, rows, None), moments, moments, factors, P(), P()),
         out_specs=(moments, moments, moments, factors),
         check_vma=False,
     )

time: 125 us -> 122 us (0.976)
  waiting for transfers between devices: 37.4 us -> 33.4 us
  starting transfers between devices: 39.3 us -> 41.4 us
  blocking collectives: 30.3 us -> 28.8 us
    ppermute x2, waiting for transfers between devices: 4.88 us -> 0.97 us  [the longest x1 0.96 us: per_device(): crossed = lax.ppermute(came_back[1], 'core', [(0, 1), (1, 0)])]
    ppermute x2, starting transfers between devices: 5.14 us -> 7.25 us  [the longest x1 5.06 us: per_device(): crossed = lax.ppermute(came_back[1], 'core', [(0, 1), (1, 0)])]
    all_to_all x1, blocking collectives: 30.3 us -> 28.8 us  [per_device(): lax.all_to_all(outgoing.reshape(2, OWNERS, ROWS, COLS), ('pair', 'chip'),...]
where the time goes in v4:
time: 122 us
  starting transfers between devices  41.4 us (34%)
  waiting for transfers between devices  33.4 us (27%)
  blocking collectives  28.8 us (24%)
  Pallas kernels  15.8 us (13%)
  local copies, waits for them, and re-layouts  1.34 us (1%)
    all_to_all x1, blocking collectives, per_device(): lax.all_to_all(outgoing.reshape(2, OWNERS, ROWS, COLS), ('pair', 'chip'),...  28.8 us
    all_to_all x1, starting transfers between devices, per_device(): lax.all_to_all(outgoing.reshape(CHIPS, GROUP // 2, 2, COLS), 'chip', 0, 0...  21.3 us
    all_to_all x1, waiting for transfers between devices, per_device(): lax.all_to_all(outgoing.reshape(CHIPS, GROUP // 2, 2, COLS), 'chip', 0, 0...  16.8 us
    all_to_all x1, waiting for transfers between devices, per_device(): chunks = lax.all_to_all(spread, ('core', 'pair', 'side'), 0, 0, tiled=True)  9.64 us
    all_to_all x1, starting transfers between devices, per_device(): chunks = lax.all_to_all(spread, ('core', 'pair', 'side'), 0, 0, tiled=True)  7.63 us
    pallas_call x1, Pallas kernels, per_device(): call(owner_kernel, [SMEM, VMEM, VMEM, VMEM], [(VMEM, (square, F32)), (VME...  6.96 us
    all_to_all x1, waiting for transfers between devices, per_device(): lax.all_to_all(partial_cols, ('pair', 'side'), 0, 0, tiled=True)  5.95 us
    all_to_all x1, starting transfers between devices, per_device(): lax.all_to_all(partial_cols, ('pair', 'side'), 0, 0, tiled=True)  5.16 us
  transfers between devices with their start and end apart: 5, of which 4 were waited for; matrix products, arithmetic and copies ran while one was open for 0% of the time, Pallas kernels for 3%

profile of v4, /device:TPU:1, one launch (start us, length us, event | category | flops | bytes accessed | tf_op | source)
XLA Modules:
  0.0 121.6 jit_solution(3990439596056905808)
XLA Ops:
  0.6 0.0 copy-start.1
  0.6 1.1 copy-done.1
  1.8 1.2 shard_map.93
  3.0 0.0 copy-start.4
  3.0 0.0 copy-start.5
  3.0 0.0 copy-start.2
  3.0 0.0 copy-start.3
  3.0 5.2 %all-to-all-start = ((bf16[4,192,4,128]{3,2,1,0:T(4,128)(2,1)}), bf16[4,192,4,128]{3,2,1,0:T(4,128)(2,1)S(1)}, u32[]{:S(2)}, u32[]{:S(2)}) async-start(bf16[4,192,4,128]{3,2,1,0:T(4,128)(2,1)} %shard_map.93), calls=%async_computation | async-start | bytes 1572864 | tf_op jit(solution)/shard_map/all_to_all | solution.py:285
  8.2 0.0 copy-done.4
  8.2 0.0 copy-done.5
  8.2 2.4 %shard_map.94.table = s32[512]{0:T(512)S(1)} custom-call(s32[192]{0:T(256)S(1)} %copy-done.4, s32[128]{0:T(128)S(1)} %copy-done.5), custom_call_target="tpu_custom_call" | custom-call | bytes 8000000 | tf_op jit(solution)/shard_map/pallas_call | solution.py:282
  10.6 6.0 %all-to-all-done = bf16[4,192,4,128]{3,2,1,0:T(4,128)(2,1)S(1)} async-done(((bf16[4,192,4,128]{3,2,1,0:T(4,128)(2,1)}), bf16[4,192,4,128]{3,2,1,0:T(4,128)(2,1)S(1)}, u32[]{:S(2)}, u32[]{:S(2)}) %all-to-all-start) | async-done | bytes 786464 | tf_op jit(solution)/shard_map/all_to_all | solution.py:285
  16.5 0.0 copy-done.2
  16.5 0.0 copy-done.3
  16.5 2.6 %shard_map.95 = (f32[768,128]{1,0:T(8,128)}, f32[768,128]{1,0:T(8,128)}, bf16[1152,128]{1,0:T(8,128)(2,1)}) custom-call(s32[512]{0:T(512)S(1)} %shard_map.94.table, bf16[4,768,128]{2,1,0:T(8,128)(2,1)S(1)} %bitcast.16, f32[768,128]{1,0:T(8,128)S(1)} %bitcast.22, f32[768,128]{1,0:T(8,128)S(1)} %bitcast.23), custom_call_target="tpu_custom_call" | custom-call | flops 4000000 | bytes 2800000 | tf_op jit(solution)/shard_map/pallas_call | solution.py:290
  19.1 21.3 %all-to-all-start.1 = ((bf16[64,9,2,128]{3,2,1,0:T(2,128)(2,1)}), bf16[64,9,2,128]{3,2,1,0:T(2,128)(2,1)S(1)}, u32[]{:S(2)}, u32[]{:S(2)}) async-start(bf16[64,9,2,128]{3,2,1,0:T(2,128)(2,1)} %bitcast.7), calls=%async_computation.1 | async-start | bytes 589824 | tf_op jit(solution)/shard_map/all_to_all | solution.py:311
  40.5 0.0 copy-done
  40.5 0.1 convert_element_type.3
  40.5 2.2 %collective-permute-start = (bf16[512,512]{1,0:T(8,128)(2,1)S(1)}, bf16[512,512]{1,0:T(8,128)(2,1)S(1)}, u32[]{:S(2)}, u32[]{:S(2)}) collective-permute-start(bf16[512,512]{1,0:T(8,128)(2,1)S(1)} %convert_element_type.3), channel_id=1, source_target_pairs={{0,1},{1,0},{2,3},{3,2},{4,5},{5,4},{6,7},{7,6},{8,9},{9,8},{10,11... | collective-permute-start | bytes 1572872 | tf_op jit(solution)/shard_map/ppermute | solution.py:288
  42.7 16.8 %all-to-all-done.1 = bf16[64,9,2,128]{3,2,1,0:T(2,128)(2,1)S(1)} async-done(((bf16[64,9,2,128]{3,2,1,0:T(2,128)(2,1)}), bf16[64,9,2,128]{3,2,1,0:T(2,128)(2,1)S(1)}, u32[]{:S(2)}, u32[]{:S(2)}) %all-to-all-start.1) | async-done | bytes 294944 | tf_op jit(solution)/shard_map/all_to_all | solution.py:311
  59.6 0.9 shard_map.96
  60.5 7.6 %all-to-all-start.2 = ((bf16[8,272,128]{2,1,0:T(8,128)(2,1)}), bf16[8,272,128]{2,1,0:T(8,128)(2,1)S(1)}, u32[]{:S(2)}, u32[]{:S(2)}) async-start(bf16[8,272,128]{2,1,0:T(8,128)(2,1)} %shard_map.96), calls=%async_computation.2 | async-start | bytes 1114112 | tf_op jit(solution)/shard_map/all_to_all | solution.py:321
  68.2 0.1 pad_add_fusion.place_ref
  68.2 0.0 collective-permute-done.other
  68.2 9.6 %all-to-all-done.2.chunks = bf16[8,272,128]{2,1,0:T(8,128)(2,1)S(1)} async-done(((bf16[8,272,128]{2,1,0:T(8,128)(2,1)}), bf16[8,272,128]{2,1,0:T(8,128)(2,1)S(1)}, u32[]{:S(2)}, u32[]{:S(2)}) %all-to-all-start.2) | async-done | bytes 557088 | tf_op jit(solution)/shard_map/all_to_all | solution.py:321
  77.9 7.0 %shard_map.97 = (f32[512,512]{1,0:T(8,128)}, bf16[2,512,128]{2,1,0:T(8,128)(2,1)S(1)}) custom-call(s32[2]{0:T(128)S(1)} %pad_add_fusion.place_ref, bf16[8,272,128]{2,1,0:T(8,128)(2,1)S(1)} %all-to-all-done.2.chunks, f32[512,512]{1,0:T(8,128)S(1)} %bitcast.19, bf16[512,512]{1,0:T(8,128)(2,1)S(1)} %collective-permute-done.other), custom_call_target="tpu_custom_call" | custom-call | flops 5000000000 | bytes 4000000 | tf_op jit(solution)/shard_map/pallas_call | solution.py:324
  84.8 0.1 copy.10
  84.9 28.8 %all_to_all.20 = bf16[2,128,4,128]{3,2,0,1:T(4,128)(2,1)S(1)} all-to-all(bf16[2,128,4,128]{3,2,0,1:T(4,128)(2,1)S(1)} %copy.10), channel_id=1, replica_groups=mesh['chip'=64,'core'=2,'pair'=2,'side'=2] {'pair','chip'}, dimensions={1} | all-to-all | bytes 524288 | tf_op jit(solution)/shard_map/all_to_all | solution.py:346
  113.8 0.1 fusion
  113.9 5.1 %collective-permute-start.1 = (bf16[512,128]{1,0:T(8,128)(2,1)S(1)}, bf16[512,128]{1,0:T(8,128)(2,1)S(1)}, u32[]{:S(2)}, u32[]{:S(2)}) collective-permute-start(bf16[512,128]{1,0:T(8,128)(2,1)S(1)} %bitcast.26), channel_id=1, source_target_pairs={{0,4},{4,0},{1,5},{5,1},{2,6},{6,2},{3,7},{7,3},{8,12},{12,8},{9,1... | collective-permute-start | bytes 393224 | tf_op jit(solution)/shard_map/ppermute | solution.py:348
  119.0 1.0 collective-permute-done.1.crossed
  119.9 1.7 %shard_map.98 = bf16[768,128]{1,0:T(8,128)(2,1)} custom-call(s32[512]{0:T(512)S(1)} %shard_map.94.table, s32[2]{0:T(128)S(1)} %pad_add_fusion.place_ref, bf16[512,128]{1,0:T(8,128)(2,1)S(1)} %bitcast.21, bf16[512,128]{1,0:T(8,128)(2,1)S(1)} %collective-permute-done.1.crossed), custom_call_target="tpu_custom_call" | custom-call | flops 1000000 | bytes 500000 | tf_op jit(solution)/shard_map/pallas_call | solution.py:349
  (1 shorter events, 0.0 us)
Async XLA Ops:
  0.6 1.1 copy-start.1
  3.0 5.2 %copy-start.4 = (s32[192]{0:T(256)S(1)}, s32[192]{0:T(256)}, u32[]{:S(2)}) copy-start(s32[192]{0:T(256)} %order) | copy-start | bytes 2308
  3.0 5.2 %copy-start.5 = (s32[128]{0:T(128)S(1)}, s32[128]{0:T(128)}, u32[]{:S(2)}) copy-start(s32[128]{0:T(128)} %counts) | copy-start | bytes 1540
  3.0 13.5 %copy-start.2 = (f32[192,4,128]{2,1,0:T(4,128)S(1)}, f32[192,4,128]{2,1,0:T(4,128)}, u32[]{:S(2)}) copy-start(f32[192,4,128]{2,1,0:T(4,128)} %param.7) | copy-start | bytes 1179652
  3.0 13.5 %copy-start.3 = (f32[192,4,128]{2,1,0:T(4,128)S(1)}, f32[192,4,128]{2,1,0:T(4,128)}, u32[]{:S(2)}) copy-start(f32[192,4,128]{2,1,0:T(4,128)} %param.8) | copy-start | bytes 1179652
  3.0 13.5 %all-to-all-start = ((bf16[4,192,4,128]{3,2,1,0:T(4,128)(2,1)}), bf16[4,192,4,128]{3,2,1,0:T(4,128)(2,1)S(1)}, u32[]{:S(2)}, u32[]{:S(2)}) async-start(bf16[4,192,4,128]{3,2,1,0:T(4,128)(2,1)} %shard_map.93), calls=%async_computation | async-start | bytes 1572864 | tf_op jit(solution)/shard_map/all_to_all | solution.py:285
  16.5 23.9 %copy-start = (f32[1,1,512,512]{3,2,1,0:T(8,128)S(1)}, f32[1,1,512,512]{3,2,1,0:T(8,128)}, u32[]{:S(2)}) copy-start(f32[1,1,512,512]{3,2,1,0:T(8,128)} %param.9) | copy-start | bytes 3145732
  19.1 40.5 %all-to-all-start.1 = ((bf16[64,9,2,128]{3,2,1,0:T(2,128)(2,1)}), bf16[64,9,2,128]{3,2,1,0:T(2,128)(2,1)S(1)}, u32[]{:S(2)}, u32[]{:S(2)}) async-start(bf16[64,9,2,128]{3,2,1,0:T(2,128)(2,1)} %bitcast.7), calls=%async_computation.1 | async-start | bytes 589824 | tf_op jit(solution)/shard_map/all_to_all | solution.py:311
  40.5 27.7 %collective-permute-start = (bf16[512,512]{1,0:T(8,128)(2,1)S(1)}, bf16[512,512]{1,0:T(8,128)(2,1)S(1)}, u32[]{:S(2)}, u32[]{:S(2)}) collective-permute-start(bf16[512,512]{1,0:T(8,128)(2,1)S(1)} %convert_element_type.3), channel_id=1, source_target_pairs={{0,1},{1,0},{2,3},{3,2},{4,5},{5,4},{6,7},{7,6},{8,9},{9,8},{10,11... | collective-permute-start | bytes 1572872 | tf_op jit(solution)/shard_map/ppermute | solution.py:288
  60.5 17.4 %all-to-all-start.2 = ((bf16[8,272,128]{2,1,0:T(8,128)(2,1)}), bf16[8,272,128]{2,1,0:T(8,128)(2,1)S(1)}, u32[]{:S(2)}, u32[]{:S(2)}) async-start(bf16[8,272,128]{2,1,0:T(8,128)(2,1)} %shard_map.96), calls=%async_computation.2 | async-start | bytes 1114112 | tf_op jit(solution)/shard_map/all_to_all | solution.py:321
  113.9 6.0 %collective-permute-start.1 = (bf16[512,128]{1,0:T(8,128)(2,1)S(1)}, bf16[512,128]{1,0:T(8,128)(2,1)S(1)}, u32[]{:S(2)}, u32[]{:S(2)}) collective-permute-start(bf16[512,128]{1,0:T(8,128)(2,1)S(1)} %bitcast.26), channel_id=1, source_target_pairs={{0,4},{4,0},{1,5},{5,1},{2,6},{6,2},{3,7},{7,3},{8,12},{12,8},{9,1... | collective-permute-start | bytes 393224 | tf_op jit(solution)/shard_map/ppermute | solution.py:348

commit v5 on v4

--- a/solution.py
+++ b/solution.py
@@ -278,7 +278,9 @@
         0,
         1_600_000,
     )(grad_parts[0])
-    partial_cols, block_order, owner_counts = lax.optimization_barrier((partial_cols, block_order, owner_counts))
+    partial_cols, block_order, owner_counts, place = lax.optimization_barrier(
+        (partial_cols, block_order, owner_counts, place)
+    )
     (table,) = call(table_kernel, [SMEM, SMEM], [(SMEM, ((4 * OWNERS,), jnp.int32))], [], 16, 0, 8_000_000)(
         block_order, owner_counts
     )
@@ -318,6 +320,7 @@
         1_000_000,
         900_000,
     )(arrived.reshape(CHIPS * GROUP, COLS))
+    spread, other_factor = lax.optimization_barrier((spread, other_factor))
     chunks = lax.all_to_all(spread, ("core", "pair", "side"), 0, 0, tiled=True)
 
     square = (ORDER, ORDER)

time: 122 us -> 122 us (level)
  blocking collectives: 28.8 us -> 47.1 us
  waiting for transfers between devices: 33.4 us -> 23.8 us
  starting transfers between devices: 41.4 us -> 33.7 us
    all_to_all x0 -> x1, blocking collectives: none -> 16.7 us  [per_device(): chunks = lax.all_to_all(spread, ('core', 'pair', 'side'), 0, 0, tiled=True)]
    all_to_all x1 -> x0, waiting for transfers between devices: 9.64 us -> none  [per_device(): chunks = lax.all_to_all(spread, ('core', 'pair', 'side'), 0, 0, tiled=True)]
    all_to_all x1 -> x0, starting transfers between devices: 7.63 us -> none  [per_device(): chunks = lax.all_to_all(spread, ('core', 'pair', 'side'), 0, 0, tiled=True)]
    all_to_all x1, blocking collectives: 28.8 us -> 30.4 us  [per_device(): lax.all_to_all(outgoing.reshape(2, OWNERS, ROWS, COLS), ('pair', 'chip'),...]
  transfers between devices with their start and end apart: 5 -> 4, of which waited for: 4 -> 3; matrix products, arithmetic and copies ran while one was open for 0% -> 0% of each run, Pallas kernels for 3% -> 2%
where the time goes in v5:
time: 122 us
  blocking collectives  47.1 us (39%)
  starting transfers between devices  33.7 us (28%)
  waiting for transfers between devices  23.8 us (20%)
  Pallas kernels  15 us (12%)
  local copies, waits for them, and re-layouts  1.33 us (1%)
    all_to_all x1, blocking collectives, per_device(): lax.all_to_all(outgoing.reshape(2, OWNERS, ROWS, COLS), ('pair', 'chip'),...  30.4 us
    all_to_all x1, starting transfers between devices, per_device(): lax.all_to_all(outgoing.reshape(CHIPS, GROUP // 2, 2, COLS), 'chip', 0, 0...  21.3 us
    all_to_all x1, waiting for transfers between devices, per_device(): lax.all_to_all(outgoing.reshape(CHIPS, GROUP // 2, 2, COLS), 'chip', 0, 0...  16.8 us
    all_to_all x1, blocking collectives, per_device(): chunks = lax.all_to_all(spread, ('core', 'pair', 'side'), 0, 0, tiled=True)  16.7 us
    pallas_call x1, Pallas kernels, per_device(): call(owner_kernel, [SMEM, VMEM, VMEM, VMEM], [(VMEM, (square, F32)), (VME...  6.95 us
    all_to_all x1, waiting for transfers between devices, per_device(): lax.all_to_all(partial_cols, ('pair', 'side'), 0, 0, tiled=True)  5.95 us
    all_to_all x1, starting transfers between devices, per_device(): lax.all_to_all(partial_cols, ('pair', 'side'), 0, 0, tiled=True)  5.16 us
    ppermute x1, starting transfers between devices, per_device(): crossed = lax.ppermute(came_back[1], 'core', [(0, 1), (1, 0)])  4.98 us
  transfers between devices with their start and end apart: 4, of which 3 were waited for; matrix products, arithmetic and copies ran while one was open for 0% of the time, Pallas kernels for 2%

profile of v5, /device:TPU:1, one launch (start us, length us, event | category | flops | bytes accessed | tf_op | source)
XLA Modules:
  0.0 121.7 jit_solution(5126392600761073500)
XLA Ops:
  0.6 0.0 copy-start.1
  0.6 1.1 copy-done.1
  1.8 1.2 shard_map.93
  3.0 0.1 pad_add_fusion.place_ref
  3.0 0.0 copy-start.4
  3.1 0.0 copy-start.5
  3.1 0.0 copy-start.2
  3.1 0.0 copy-start.3
  3.1 5.2 %all-to-all-start = ((bf16[4,192,4,128]{3,2,1,0:T(4,128)(2,1)}), bf16[4,192,4,128]{3,2,1,0:T(4,128)(2,1)S(1)}, u32[]{:S(2)}, u32[]{:S(2)}) async-start(bf16[4,192,4,128]{3,2,1,0:T(4,128)(2,1)} %shard_map.93), calls=%async_computation | async-start | bytes 1572864 | tf_op jit(solution)/shard_map/all_to_all | solution.py:287
  8.2 0.0 copy-done.4
  8.2 0.0 copy-done.5
  8.2 2.4 %shard_map.94.table = s32[512]{0:T(512)S(1)} custom-call(s32[192]{0:T(256)S(1)} %copy-done.4, s32[128]{0:T(128)S(1)} %copy-done.5), custom_call_target="tpu_custom_call" | custom-call | bytes 8000000 | tf_op jit(solution)/shard_map/pallas_call | solution.py:284
  10.6 6.0 %all-to-all-done = bf16[4,192,4,128]{3,2,1,0:T(4,128)(2,1)S(1)} async-done(((bf16[4,192,4,128]{3,2,1,0:T(4,128)(2,1)}), bf16[4,192,4,128]{3,2,1,0:T(4,128)(2,1)S(1)}, u32[]{:S(2)}, u32[]{:S(2)}) %all-to-all-start) | async-done | bytes 786464 | tf_op jit(solution)/shard_map/all_to_all | solution.py:287
  16.6 0.0 copy-done.2
  16.6 0.0 copy-done.3
  16.6 0.0 copy-start
  16.6 2.6 %shard_map.95 = (f32[768,128]{1,0:T(8,128)}, f32[768,128]{1,0:T(8,128)}, bf16[1152,128]{1,0:T(8,128)(2,1)}) custom-call(s32[512]{0:T(512)S(1)} %shard_map.94.table, bf16[4,768,128]{2,1,0:T(8,128)(2,1)S(1)} %bitcast.16, f32[768,128]{1,0:T(8,128)S(1)} %bitcast.22, f32[768,128]{1,0:T(8,128)S(1)} %bitcast.23), custom_call_target="tpu_custom_call" | custom-call | flops 4000000 | bytes 2800000 | tf_op jit(solution)/shard_map/pallas_call | solution.py:292
  19.2 21.3 %all-to-all-start.1 = ((bf16[64,9,2,128]{3,2,1,0:T(2,128)(2,1)}), bf16[64,9,2,128]{3,2,1,0:T(2,128)(2,1)S(1)}, u32[]{:S(2)}, u32[]{:S(2)}) async-start(bf16[64,9,2,128]{3,2,1,0:T(2,128)(2,1)} %bitcast.7), calls=%async_computation.1 | async-start | bytes 589824 | tf_op jit(solution)/shard_map/all_to_all | solution.py:313
  40.5 0.0 copy-done
  40.5 0.1 convert_element_type.3
  40.6 2.2 %collective-permute-start = (bf16[512,512]{1,0:T(8,128)(2,1)S(1)}, bf16[512,512]{1,0:T(8,128)(2,1)S(1)}, u32[]{:S(2)}, u32[]{:S(2)}) collective-permute-start(bf16[512,512]{1,0:T(8,128)(2,1)S(1)} %convert_element_type.3), channel_id=1, source_target_pairs={{0,1},{1,0},{2,3},{3,2},{4,5},{5,4},{6,7},{7,6},{8,9},{9,8},{10,11... | collective-permute-start | bytes 1572872 | tf_op jit(solution)/shard_map/ppermute | solution.py:290
  42.8 16.8 %all-to-all-done.1 = bf16[64,9,2,128]{3,2,1,0:T(2,128)(2,1)S(1)} async-done(((bf16[64,9,2,128]{3,2,1,0:T(2,128)(2,1)}), bf16[64,9,2,128]{3,2,1,0:T(2,128)(2,1)S(1)}, u32[]{:S(2)}, u32[]{:S(2)}) %all-to-all-start.1) | async-done | bytes 294944 | tf_op jit(solution)/shard_map/all_to_all | solution.py:313
  59.6 0.1 shard_map.96
  59.8 0.0 collective-permute-done.other
  59.8 16.7 %all_to_all.20.chunks = bf16[8,272,128]{2,1,0:T(8,128)(2,1)S(1)} all-to-all(bf16[8,272,128]{2,1,0:T(8,128)(2,1)S(1)} %shard_map.96), channel_id=1, replica_groups=mesh['chip'=64,'core'=2,'pair'=2,'side'=2] {'core','pair','side'}, dimensions={0} | all-to-all | bytes 1114112 | tf_op jit(solution)/shard_map/all_to_all | solution.py:324
  76.5 7.0 %shard_map.97 = (f32[512,512]{1,0:T(8,128)}, bf16[2,512,128]{2,1,0:T(8,128)(2,1)S(1)}) custom-call(s32[2]{0:T(128)S(1)} %pad_add_fusion.place_ref, bf16[8,272,128]{2,1,0:T(8,128)(2,1)S(1)} %all_to_all.20.chunks, f32[512,512]{1,0:T(8,128)S(1)} %bitcast.19, bf16[512,512]{1,0:T(8,128)(2,1)S(1)} %collective-permute-done.other), custom_call_target="tpu_custom_call" | custom-call | flops 5000000000 | bytes 4000000 | tf_op jit(solution)/shard_map/pallas_call | solution.py:327
  83.5 0.1 copy.10
  83.6 30.4 %all_to_all.21 = bf16[2,128,4,128]{3,2,0,1:T(4,128)(2,1)S(1)} all-to-all(bf16[2,128,4,128]{3,2,0,1:T(4,128)(2,1)S(1)} %copy.10), channel_id=1, replica_groups=mesh['chip'=64,'core'=2,'pair'=2,'side'=2] {'pair','chip'}, dimensions={1} | all-to-all | bytes 524288 | tf_op jit(solution)/shard_map/all_to_all | solution.py:349
  113.9 0.1 fusion
  114.0 5.0 %collective-permute-start.1 = (bf16[512,128]{1,0:T(8,128)(2,1)S(1)}, bf16[512,128]{1,0:T(8,128)(2,1)S(1)}, u32[]{:S(2)}, u32[]{:S(2)}) collective-permute-start(bf16[512,128]{1,0:T(8,128)(2,1)S(1)} %bitcast.26), channel_id=1, source_target_pairs={{0,4},{4,0},{1,5},{5,1},{2,6},{6,2},{3,7},{7,3},{8,12},{12,8},{9,1... | collective-permute-start | bytes 393224 | tf_op jit(solution)/shard_map/ppermute | solution.py:351
  119.0 1.0 collective-permute-done.1.crossed
  120.0 1.7 %shard_map.98 = bf16[768,128]{1,0:T(8,128)(2,1)} custom-call(s32[512]{0:T(512)S(1)} %shard_map.94.table, s32[2]{0:T(128)S(1)} %pad_add_fusion.place_ref, bf16[512,128]{1,0:T(8,128)(2,1)S(1)} %bitcast.21, bf16[512,128]{1,0:T(8,128)(2,1)S(1)} %collective-permute-done.1.crossed), custom_call_target="tpu_custom_call" | custom-call | flops 1000000 | bytes 500000 | tf_op jit(solution)/shard_map/pallas_call | solution.py:352
Async XLA Ops:
  0.6 1.1 copy-start.1
  3.0 5.2 %copy-start.4 = (s32[192]{0:T(256)S(1)}, s32[192]{0:T(256)}, u32[]{:S(2)}) copy-start(s32[192]{0:T(256)} %order) | copy-start | bytes 2308
  3.1 5.2 %copy-start.5 = (s32[128]{0:T(128)S(1)}, s32[128]{0:T(128)}, u32[]{:S(2)}) copy-start(s32[128]{0:T(128)} %counts) | copy-start | bytes 1540
  3.1 13.5 %copy-start.2 = (f32[192,4,128]{2,1,0:T(4,128)S(1)}, f32[192,4,128]{2,1,0:T(4,128)}, u32[]{:S(2)}) copy-start(f32[192,4,128]{2,1,0:T(4,128)} %param.7) | copy-start | bytes 1179652
  3.1 13.5 %copy-start.3 = (f32[192,4,128]{2,1,0:T(4,128)S(1)}, f32[192,4,128]{2,1,0:T(4,128)}, u32[]{:S(2)}) copy-start(f32[192,4,128]{2,1,0:T(4,128)} %param.8) | copy-start | bytes 1179652
  3.1 13.5 %all-to-all-start = ((bf16[4,192,4,128]{3,2,1,0:T(4,128)(2,1)}), bf16[4,192,4,128]{3,2,1,0:T(4,128)(2,1)S(1)}, u32[]{:S(2)}, u32[]{:S(2)}) async-start(bf16[4,192,4,128]{3,2,1,0:T(4,128)(2,1)} %shard_map.93), calls=%async_computation | async-start | bytes 1572864 | tf_op jit(solution)/shard_map/all_to_all | solution.py:287
  16.6 23.9 %copy-start = (f32[1,1,512,512]{3,2,1,0:T(8,128)S(1)}, f32[1,1,512,512]{3,2,1,0:T(8,128)}, u32[]{:S(2)}) copy-start(f32[1,1,512,512]{3,2,1,0:T(8,128)} %param.9) | copy-start | bytes 3145732
  19.2 40.5 %all-to-all-start.1 = ((bf16[64,9,2,128]{3,2,1,0:T(2,128)(2,1)}), bf16[64,9,2,128]{3,2,1,0:T(2,128)(2,1)S(1)}, u32[]{:S(2)}, u32[]{:S(2)}) async-start(bf16[64,9,2,128]{3,2,1,0:T(2,128)(2,1)} %bitcast.7), calls=%async_computation.1 | async-start | bytes 589824 | tf_op jit(solution)/shard_map/all_to_all | solution.py:313
  40.6 19.2 %collective-permute-start = (bf16[512,512]{1,0:T(8,128)(2,1)S(1)}, bf16[512,512]{1,0:T(8,128)(2,1)S(1)}, u32[]{:S(2)}, u32[]{:S(2)}) collective-permute-start(bf16[512,512]{1,0:T(8,128)(2,1)S(1)} %convert_element_type.3), channel_id=1, source_target_pairs={{0,1},{1,0},{2,3},{3,2},{4,5},{5,4},{6,7},{7,6},{8,9},{9,8},{10,11... | collective-permute-start | bytes 1572872 | tf_op jit(solution)/shard_map/ppermute | solution.py:290
  114.0 6.0 %collective-permute-start.1 = (bf16[512,128]{1,0:T(8,128)(2,1)S(1)}, bf16[512,128]{1,0:T(8,128)(2,1)S(1)}, u32[]{:S(2)}, u32[]{:S(2)}) collective-permute-start(bf16[512,128]{1,0:T(8,128)(2,1)S(1)} %bitcast.26), channel_id=1, source_target_pairs={{0,4},{4,0},{1,5},{5,1},{2,6},{6,2},{3,7},{7,3},{8,12},{12,8},{9,1... | collective-permute-start | bytes 393224 | tf_op jit(solution)/shard_map/ppermute | solution.py:351

commit v6 on v5

--- a/solution.py
+++ b/solution.py
@@ -154,8 +154,8 @@
 def owner_kernel(
     place_ref, chunks, mine, other, new_mine, outgoing, grad, stats, lefts, rights, later, squares, outer, cubes, roots, inner, result
 ):
-    here, core = place_ref[0], place_ref[1]
-    is_right = here == 1
+    core, front = place_ref[1], place_ref[2]
+    is_right = place_ref[0] == 1
     halves = [slice(0, ORDER // 2), slice(ORDER // 2, ORDER)]
     for n in range(NARROW):
         rows = [chunks[NARROW * core + n, 0:HALF].astype(F32).reshape(CHIPS, ROWS, COLS) for core in range(CORES)]
@@ -224,7 +224,8 @@
     square = sum_of_squares([result[rows] for rows in halves])
     scale = jnp.sqrt(adam_sq) / (jnp.sqrt(square) + 1e-06)
     for pair in range(2):
-        cols = result[:, pl.ds(pl.multiple_of((2 * pair + here) * COLS, COLS), COLS)] * scale
+        member = front if pair == 0 else NARROW - 1 - front
+        cols = result[:, pl.ds(pl.multiple_of(member * COLS, COLS), COLS)] * scale
         cols = cols.reshape(CHIPS, CORES * ROWS, COLS)
         lower, upper = cols[:, 0:ROWS], cols[:, ROWS : 2 * ROWS]
         staying = jnp.where(core == 0, lower, upper).reshape(HALF, COLS)
@@ -266,7 +267,11 @@
 
 
 def per_device(grad_parts, first_moment, second_moment, factors, block_order, owner_counts):
-    place = jnp.stack([lax.axis_index("side"), lax.axis_index("core")]).astype(jnp.int32)
+    pair, side, core = (lax.axis_index(name) for name in ("pair", "side", "core"))
+    front = jnp.where(pair == 0, side, 1 - side)
+    place = jnp.stack([side, core, front]).astype(jnp.int32)
+    index = [[member * CHIPS + chip for chip in range(CHIPS)] for member in range(NARROW)]
+    sharing = [index[0] + index[3], index[1] + index[2]]
     flat = BLOCKS * ROWS
 
     (partial_cols,) = call(
@@ -346,7 +351,14 @@
         4_000_000,
     )(place, chunks, factor, other_factor)
 
-    came_back = lax.all_to_all(outgoing.reshape(2, OWNERS, ROWS, COLS), ("pair", "chip"), 1, 1, tiled=True)
+    came_back = lax.all_to_all(
+        outgoing.reshape(2, OWNERS, ROWS, COLS),
+        ("pair", "side", "chip"),
+        1,
+        1,
+        axis_index_groups=sharing,
+        tiled=True,
+    )
     came_back = came_back.reshape(2, ORDER, COLS)
     crossed = lax.ppermute(came_back[1], "core", [(0, 1), (1, 0)])
     (update,) = call(

time: 122 us -> 122 us (level)
  no operation moved by 1% of the time
where the time goes in v6:
time: 122 us; the launch traced here: 121 us
  blocking collectives  46.6 us (38%)
  starting transfers between devices  33.8 us (28%)
  waiting for transfers between devices  23.8 us (20%)
  Pallas kernels  15 us (12%)
  local copies, waits for them, and re-layouts  1.33 us (1%)
    all_to_all x1, blocking collectives, per_device(): lax.all_to_all(outgoing.reshape(2, OWNERS, ROWS, COLS), ('pair', 'side',...  29.9 us
    all_to_all x1, starting transfers between devices, per_device(): lax.all_to_all(outgoing.reshape(CHIPS, GROUP // 2, 2, COLS), 'chip', 0, 0...  21.3 us
    all_to_all x1, waiting for transfers between devices, per_device(): lax.all_to_all(outgoing.reshape(CHIPS, GROUP // 2, 2, COLS), 'chip', 0, 0...  16.8 us
    all_to_all x1, blocking collectives, per_device(): chunks = lax.all_to_all(spread, ('core', 'pair', 'side'), 0, 0, tiled=True)  16.7 us
    pallas_call x1, Pallas kernels, per_device(): call(owner_kernel, [SMEM, VMEM, VMEM, VMEM], [(VMEM, (square, F32)), (VME...  6.95 us
    all_to_all x1, waiting for transfers between devices, per_device(): lax.all_to_all(partial_cols, ('pair', 'side'), 0, 0, tiled=True)  5.95 us
    all_to_all x1, starting transfers between devices, per_device(): lax.all_to_all(partial_cols, ('pair', 'side'), 0, 0, tiled=True)  5.16 us
    ppermute x1, starting transfers between devices, per_device(): crossed = lax.ppermute(came_back[1], 'core', [(0, 1), (1, 0)])  5.15 us
  transfers between devices with their start and end apart: 4, of which 3 were waited for; matrix products, arithmetic and copies ran while one was open for 0% of the time, Pallas kernels for 2%

profile of v6, /device:TPU:1, one launch (start us, length us, event | category | flops | bytes accessed | tf_op | source)
XLA Modules:
  0.0 121.4 jit_solution(10760679618754271570)
XLA Ops:
  0.6 0.0 copy-start.1
  0.6 1.1 copy-done.1
  1.8 1.2 shard_map.93
  3.0 0.1 pad_add_fusion.place_ref
  3.1 0.0 copy-start.4
  3.1 0.0 copy-start.5
  3.1 0.0 copy-start.2
  3.1 0.0 copy-start.3
  3.1 5.2 %all-to-all-start = ((bf16[4,192,4,128]{3,2,1,0:T(4,128)(2,1)}), bf16[4,192,4,128]{3,2,1,0:T(4,128)(2,1)S(1)}, u32[]{:S(2)}, u32[]{:S(2)}) async-start(bf16[4,192,4,128]{3,2,1,0:T(4,128)(2,1)} %shard_map.93), calls=%async_computation | async-start | bytes 1572864 | tf_op jit(solution)/shard_map/all_to_all | solution.py:292
  8.2 0.0 copy-done.4
  8.2 0.0 copy-done.5
  8.2 2.4 %shard_map.94.table = s32[512]{0:T(512)S(1)} custom-call(s32[192]{0:T(256)S(1)} %copy-done.4, s32[128]{0:T(128)S(1)} %copy-done.5), custom_call_target="tpu_custom_call" | custom-call | bytes 8000000 | tf_op jit(solution)/shard_map/pallas_call | solution.py:289
  10.6 6.0 %all-to-all-done = bf16[4,192,4,128]{3,2,1,0:T(4,128)(2,1)S(1)} async-done(((bf16[4,192,4,128]{3,2,1,0:T(4,128)(2,1)}), bf16[4,192,4,128]{3,2,1,0:T(4,128)(2,1)S(1)}, u32[]{:S(2)}, u32[]{:S(2)}) %all-to-all-start) | async-done | bytes 786464 | tf_op jit(solution)/shard_map/all_to_all | solution.py:292
  16.6 0.0 copy-done.2
  16.6 0.0 copy-done.3
  16.6 0.0 copy-start
  16.6 2.6 %shard_map.95 = (f32[768,128]{1,0:T(8,128)}, f32[768,128]{1,0:T(8,128)}, bf16[1152,128]{1,0:T(8,128)(2,1)}) custom-call(s32[512]{0:T(512)S(1)} %shard_map.94.table, bf16[4,768,128]{2,1,0:T(8,128)(2,1)S(1)} %bitcast.17, f32[768,128]{1,0:T(8,128)S(1)} %bitcast.23, f32[768,128]{1,0:T(8,128)S(1)} %bitcast.24), custom_call_target="tpu_custom_call" | custom-call | flops 4000000 | bytes 2800000 | tf_op jit(solution)/shard_map/pallas_call | solution.py:297
  19.2 21.3 %all-to-all-start.1 = ((bf16[64,9,2,128]{3,2,1,0:T(2,128)(2,1)}), bf16[64,9,2,128]{3,2,1,0:T(2,128)(2,1)S(1)}, u32[]{:S(2)}, u32[]{:S(2)}) async-start(bf16[64,9,2,128]{3,2,1,0:T(2,128)(2,1)} %bitcast.8), calls=%async_computation.1 | async-start | bytes 589824 | tf_op jit(solution)/shard_map/all_to_all | solution.py:318
  40.5 0.0 copy-done
  40.5 0.1 convert_element_type.3
  40.6 2.2 %collective-permute-start = (bf16[512,512]{1,0:T(8,128)(2,1)S(1)}, bf16[512,512]{1,0:T(8,128)(2,1)S(1)}, u32[]{:S(2)}, u32[]{:S(2)}) collective-permute-start(bf16[512,512]{1,0:T(8,128)(2,1)S(1)} %convert_element_type.3), channel_id=1, source_target_pairs={{0,1},{1,0},{2,3},{3,2},{4,5},{5,4},{6,7},{7,6},{8,9},{9,8},{10,11... | collective-permute-start | bytes 1572872 | tf_op jit(solution)/shard_map/ppermute | solution.py:295
  42.8 16.8 %all-to-all-done.1 = bf16[64,9,2,128]{3,2,1,0:T(2,128)(2,1)S(1)} async-done(((bf16[64,9,2,128]{3,2,1,0:T(2,128)(2,1)}), bf16[64,9,2,128]{3,2,1,0:T(2,128)(2,1)S(1)}, u32[]{:S(2)}, u32[]{:S(2)}) %all-to-all-start.1) | async-done | bytes 294944 | tf_op jit(solution)/shard_map/all_to_all | solution.py:318
  59.6 0.1 shard_map.96
  59.8 0.0 collective-permute-done.other
  59.8 16.7 %all_to_all.20.chunks = bf16[8,272,128]{2,1,0:T(8,128)(2,1)S(1)} all-to-all(bf16[8,272,128]{2,1,0:T(8,128)(2,1)S(1)} %shard_map.96), channel_id=1, replica_groups=mesh['chip'=64,'core'=2,'pair'=2,'side'=2] {'core','pair','side'}, dimensions={0} | all-to-all | bytes 1114112 | tf_op jit(solution)/shard_map/all_to_all | solution.py:329
  76.5 7.0 %shard_map.97 = (f32[512,512]{1,0:T(8,128)}, bf16[2,512,128]{2,1,0:T(8,128)(2,1)S(1)}) custom-call(s32[3]{0:T(128)S(1)} %pad_add_fusion.place_ref, bf16[8,272,128]{2,1,0:T(8,128)(2,1)S(1)} %all_to_all.20.chunks, f32[512,512]{1,0:T(8,128)S(1)} %bitcast.20, bf16[512,512]{1,0:T(8,128)(2,1)S(1)} %collective-permute-done.other), custom_call_target="tpu_custom_call" | custom-call | flops 5000000000 | bytes 4000000 | tf_op jit(solution)/shard_map/pallas_call | solution.py:332
  83.5 0.1 copy.10
  83.6 29.9 %all_to_all.21 = bf16[2,128,4,128]{3,2,0,1:T(4,128)(2,1)S(1)} all-to-all(bf16[2,128,4,128]{3,2,0,1:T(4,128)(2,1)S(1)} %copy.10), channel_id=1, replica_groups={{0,8,16,24,32,40,48,56,64,72,80,88,96,104,112,120,128,136,144,152,160,1..., dimensions={1} | all-to-all | bytes 524288 | tf_op jit(solution)/shard_map/all_to_all | solution.py:354
  113.5 0.1 fusion
  113.6 5.2 %collective-permute-start.1 = (bf16[512,128]{1,0:T(8,128)(2,1)S(1)}, bf16[512,128]{1,0:T(8,128)(2,1)S(1)}, u32[]{:S(2)}, u32[]{:S(2)}) collective-permute-start(bf16[512,128]{1,0:T(8,128)(2,1)S(1)} %bitcast.27), channel_id=1, source_target_pairs={{0,4},{4,0},{1,5},{5,1},{2,6},{6,2},{3,7},{7,3},{8,12},{12,8},{9,1... | collective-permute-start | bytes 393224 | tf_op jit(solution)/shard_map/ppermute | solution.py:363
  118.8 1.0 collective-permute-done.1.crossed
  119.7 1.7 %shard_map.98 = bf16[768,128]{1,0:T(8,128)(2,1)} custom-call(s32[512]{0:T(512)S(1)} %shard_map.94.table, s32[3]{0:T(128)S(1)} %pad_add_fusion.place_ref, bf16[512,128]{1,0:T(8,128)(2,1)S(1)} %bitcast.22, bf16[512,128]{1,0:T(8,128)(2,1)S(1)} %collective-permute-done.1.crossed), custom_call_target="tpu_custom_call" | custom-call | flops 1000000 | bytes 500000 | tf_op jit(solution)/shard_map/pallas_call | solution.py:364
Async XLA Ops:
  0.6 1.1 copy-start.1
  3.1 5.2 %copy-start.4 = (s32[192]{0:T(256)S(1)}, s32[192]{0:T(256)}, u32[]{:S(2)}) copy-start(s32[192]{0:T(256)} %order) | copy-start | bytes 2308
  3.1 5.2 %copy-start.5 = (s32[128]{0:T(128)S(1)}, s32[128]{0:T(128)}, u32[]{:S(2)}) copy-start(s32[128]{0:T(128)} %counts) | copy-start | bytes 1540
  3.1 13.5 %copy-start.2 = (f32[192,4,128]{2,1,0:T(4,128)S(1)}, f32[192,4,128]{2,1,0:T(4,128)}, u32[]{:S(2)}) copy-start(f32[192,4,128]{2,1,0:T(4,128)} %param.7) | copy-start | bytes 1179652
  3.1 13.5 %copy-start.3 = (f32[192,4,128]{2,1,0:T(4,128)S(1)}, f32[192,4,128]{2,1,0:T(4,128)}, u32[]{:S(2)}) copy-start(f32[192,4,128]{2,1,0:T(4,128)} %param.8) | copy-start | bytes 1179652
  3.1 13.5 %all-to-all-start = ((bf16[4,192,4,128]{3,2,1,0:T(4,128)(2,1)}), bf16[4,192,4,128]{3,2,1,0:T(4,128)(2,1)S(1)}, u32[]{:S(2)}, u32[]{:S(2)}) async-start(bf16[4,192,4,128]{3,2,1,0:T(4,128)(2,1)} %shard_map.93), calls=%async_computation | async-start | bytes 1572864 | tf_op jit(solution)/shard_map/all_to_all | solution.py:292
  16.6 23.9 %copy-start = (f32[1,1,512,512]{3,2,1,0:T(8,128)S(1)}, f32[1,1,512,512]{3,2,1,0:T(8,128)}, u32[]{:S(2)}) copy-start(f32[1,1,512,512]{3,2,1,0:T(8,128)} %param.9) | copy-start | bytes 3145732
  19.2 40.5 %all-to-all-start.1 = ((bf16[64,9,2,128]{3,2,1,0:T(2,128)(2,1)}), bf16[64,9,2,128]{3,2,1,0:T(2,128)(2,1)S(1)}, u32[]{:S(2)}, u32[]{:S(2)}) async-start(bf16[64,9,2,128]{3,2,1,0:T(2,128)(2,1)} %bitcast.8), calls=%async_computation.1 | async-start | bytes 589824 | tf_op jit(solution)/shard_map/all_to_all | solution.py:318
  40.6 19.2 %collective-permute-start = (bf16[512,512]{1,0:T(8,128)(2,1)S(1)}, bf16[512,512]{1,0:T(8,128)(2,1)S(1)}, u32[]{:S(2)}, u32[]{:S(2)}) collective-permute-start(bf16[512,512]{1,0:T(8,128)(2,1)S(1)} %convert_element_type.3), channel_id=1, source_target_pairs={{0,1},{1,0},{2,3},{3,2},{4,5},{5,4},{6,7},{7,6},{8,9},{9,8},{10,11... | collective-permute-start | bytes 1572872 | tf_op jit(solution)/shard_map/ppermute | solution.py:295
  113.6 6.1 %collective-permute-start.1 = (bf16[512,128]{1,0:T(8,128)(2,1)S(1)}, bf16[512,128]{1,0:T(8,128)(2,1)S(1)}, u32[]{:S(2)}, u32[]{:S(2)}) collective-permute-start(bf16[512,128]{1,0:T(8,128)(2,1)S(1)} %bitcast.27), channel_id=1, source_target_pairs={{0,4},{4,0},{1,5},{5,1},{2,6},{6,2},{3,7},{7,3},{8,12},{12,8},{9,1... | collective-permute-start | bytes 393224 | tf_op jit(solution)/shard_map/ppermute | solution.py:363
